TPU v7x, 32 devices: a whole 2x2x4 slice. The times are simulated.
32 devices in a mesh: fsdp: 4 (over y, x), tensor: 8 (over z, core).
Axes of the slice: x: 2, y: 2, z: 4, core: 2. Of those that a mesh axis runs over, the one named last changes fastest.
Arguments:
- tokens: bfloat16 [768, 8192], P(('fsdp', 'tensor')), may hold values from -6 to 6
- out_grad: bfloat16 [768, 8192], P(('fsdp', 'tensor')), may hold values from -6 to 6
- up_weight: bfloat16 [256, 8, 128, 128], P('tensor', 'fsdp'), may hold values from -0.1875 to 0.1875
- down_weight: bfloat16 [256, 8, 128, 128], P('tensor', 'fsdp'), may hold values from -0.09375 to 0.09375
- up_index: int32 [256, 8], P('tensor'), may hold values from 0 to 63, all different within a row
- down_index: int32 [256, 8], P('tensor'), may hold values from 0 to 63, all different within a row
Outputs:
- mixed: bfloat16 [768, 8192], P(('fsdp', 'tensor'))
- input_grad: bfloat16 [768, 8192], P(('fsdp', 'tensor'))
- up_grad: float32 [256, 8, 128, 128], P('tensor', 'fsdp')
- down_grad: float32 [256, 8, 128, 128], P('tensor', 'fsdp')
Inputs may be any that keep to these rules, and one draw needn't show every extreme that they name: Each row of up_index names 8 different input blocks; every block is named somewhere. Each row of down_index names 8 different output blocks; every block is named somewhere.
All inputs are finite; a program needn't handle non-finite values.
Results may differ from a plain program's by a relative error of at most 0.024.
Values may be sent and summed in bfloat16 or wider, within the bound.
No kernel may reach another device: no remote copies, remote signals or barrier semaphores. Data moves between devices by JAX's collectives and lax.ppermute only.
A program may use at most 192 MiB of HBM per device.

v0:
```python
import functools

import jax
import jax.numpy as jnp
from jax import lax
from jax.experimental import pallas as pl
from jax.experimental.pallas import tpu as pltpu
from jax.sharding import PartitionSpec as P

BLK = 128
CHUNKS = 4
MIB = 1 << 20
NT = (((1,), (1,)), ((), ()))
TN = (((0,), (0,)), ((), ()))


def dot(a, b, dims=(((1,), (0,)), ((), ()))):
    return lax.dot_general(a, b, dims, preferred_element_type=jnp.float32)


def columns(ref, blocks, offset=0):
    parts = [ref[:, pl.ds(pl.multiple_of(b * BLK + offset, BLK), BLK)] for b in blocks]
    return parts[0] if len(parts) == 1 else jnp.concatenate(parts, axis=1)


def side_by_side(ref, j, slots):
    parts = [ref[j, s] for s in range(slots)]
    return parts[0] if len(parts) == 1 else jnp.concatenate(parts, axis=1)


def forward_kernel(n, first, per_step, me_ref, up_idx, down_idx, rows_ref, *refs):
    ups, downs, out_ref = refs[:n], refs[n : 2 * n], refs[2 * n]
    slots = ups[0].shape[1]
    width = rows_ref.shape[1] // 2
    me = me_ref[0]
    for jj in range(per_step):
        j = first + pl.program_id(0) * per_step + jj
        pre = jnp.zeros((rows_ref.shape[0], BLK), jnp.float32)
        grad = jnp.zeros((rows_ref.shape[0], BLK), jnp.float32)
        for r in range(n):
            k = (me ^ r) * slots
            chosen = columns(rows_ref, [up_idx[j, k + s] for s in range(slots)])
            pre = pre + dot(chosen, ups[r][jj].reshape(slots * BLK, BLK))
            picked = columns(rows_ref, [down_idx[j, k + s] for s in range(slots)], width)
            grad = grad + dot(picked, side_by_side(downs[r], jj, slots), NT)
        sigma = jax.nn.sigmoid(pre)
        out_ref[0, jj] = (pre * sigma).astype(jnp.bfloat16)
        out_ref[1, jj] = (grad * sigma * (1.0 + pre * (1.0 - sigma))).astype(jnp.bfloat16)


def grad_kernel(n, first, per_step, me_ref, up_idx, down_idx, mine, other, h_mine, h_other, *outs):
    slots = outs[0].shape[1]
    width = mine.shape[1] // 2
    me = me_ref[0]
    for jj in range(per_step):
        j = first + pl.program_id(0) * per_step + jj
        for e, r in enumerate(range(0, n, 2)):
            k = (me ^ r) * slots
            up_cols = [up_idx[j, k + s] for s in range(slots)]
            down_cols = [down_idx[j, k + s] for s in range(slots)]
            up = dot(columns(mine, up_cols), h_mine[1, jj], TN)
            up = up + dot(columns(other, up_cols), h_other[1, jj], TN)
            down = dot(h_mine[0, jj], columns(mine, down_cols, width), TN)
            down = down + dot(h_other[0, jj], columns(other, down_cols, width), TN)
            for s in range(slots):
                up_tile = up[s * BLK : (s + 1) * BLK]
                down_tile = down[:, s * BLK : (s + 1) * BLK]
                if e == 0:
                    outs[0][jj, s] = up_tile
                    outs[1][jj, s] = down_tile
                else:
                    outs[1 + e][0, jj, s] = up_tile.astype(jnp.bfloat16)
                    outs[1 + e][1, jj, s] = down_tile.astype(jnp.bfloat16)


def spread_kernel(n, chunks, per_chunk, which, me_ref, idx, *refs):
    hs, ws = refs[:chunks], refs[chunks : chunks + chunks * n]
    out_ref, acc = refs[-2], refs[-1]
    slots = ws[0].shape[1]
    me = me_ref[0]
    step = pl.program_id(0)

    @pl.when(step == 0)
    def _():
        acc[...] = jnp.zeros_like(acc)

    for c in range(chunks):
        j = c * per_chunk + step
        h = hs[c][0, 0]
        for r in range(n):
            k = (me ^ r) * slots
            w = ws[c * n + r]
            if which == 0:
                terms = dot(h, side_by_side(w, 0, slots))
            else:
                terms = dot(h, w[0].reshape(slots * BLK, BLK), NT)
            for s in range(slots):
                at = pl.ds(pl.multiple_of(idx[j, k + s] * BLK, BLK), BLK)
                acc[:, at] += terms[:, s * BLK : (s + 1) * BLK]

    @pl.when(step == pl.num_programs(0) - 1)
    def _():
        out_ref[...] = acc[...].astype(out_ref.dtype)


def smem():
    return pl.BlockSpec(memory_space=pltpu.SMEM)


def whole(shape):
    return pl.BlockSpec(shape, lambda i: (0,) * len(shape), pipeline_mode=pl.Buffered(1))


def params():
    return pltpu.CompilerParams(vmem_limit_bytes=48 * MIB)


def forward(n, first, me, up_index, down_index, rows, ups, downs):
    per_chunk, slots = ups[0].shape[:2]
    count = rows.shape[0]
    per_step = 2
    tile = pl.BlockSpec((per_step, slots, BLK, BLK), lambda i: (i, 0, 0, 0))
    flops = 4 * count * per_chunk * slots * n * BLK * BLK
    return pl.pallas_call(
        functools.partial(forward_kernel, n, first, per_step),
        grid=(per_chunk // per_step,),
        in_specs=[smem()] * 3 + [whole(rows.shape)] + [tile] * (2 * n),
        out_specs=pl.BlockSpec((2, per_step, count, BLK), lambda i: (0, i, 0, 0)),
        out_shape=jax.ShapeDtypeStruct((2, per_chunk, count, BLK), jnp.bfloat16),
        compiler_params=params(),
        cost_estimate=pl.CostEstimate(flops=flops, bytes_accessed=10 * MIB, transcendentals=0),
        name="forward_chunk",
    )(me, up_index, down_index, rows, *ups, *downs)


def grads(n, first, me, up_index, down_index, mine, other, h_mine, h_other, slots):
    per_chunk, count = h_mine.shape[1:3]
    per_step = 2
    h_spec = pl.BlockSpec((2, per_step, count, BLK), lambda i: (0, i, 0, 0))
    own = pl.BlockSpec((per_step, slots, BLK, BLK), lambda i: (i, 0, 0, 0))
    sent = pl.BlockSpec((2, per_step, slots, BLK, BLK), lambda i: (0, i, 0, 0, 0))
    own_shape = jax.ShapeDtypeStruct((per_chunk, slots, BLK, BLK), jnp.float32)
    sent_shape = jax.ShapeDtypeStruct((2, per_chunk, slots, BLK, BLK), jnp.bfloat16)
    flops = 4 * count * per_chunk * slots * n * BLK * BLK
    return pl.pallas_call(
        functools.partial(grad_kernel, n, first, per_step),
        grid=(per_chunk // per_step,),
        in_specs=[smem()] * 3 + [whole(mine.shape)] * 2 + [h_spec] * 2,
        out_specs=[own] * 2 + [sent] * (n // 2 - 1),
        out_shape=[own_shape] * 2 + [sent_shape] * (n // 2 - 1),
        compiler_params=params(),
        cost_estimate=pl.CostEstimate(flops=flops, bytes_accessed=18 * MIB, transcendentals=0),
        name="grad_chunk",
    )(me, up_index, down_index, mine, other, h_mine, h_other)


def spread(n, which, me, index, hs, ws, width):
    chunks = len(hs)
    per_chunk, count = hs[0].shape[1:3]
    slots = ws[0][0].shape[1]
    tile = pl.BlockSpec((1, slots, BLK, BLK), lambda i: (i, 0, 0, 0))
    h_spec = pl.BlockSpec((1, 1, count, BLK), lambda i: (which, i, 0, 0))
    flops = 2 * count * per_chunk * chunks * slots * n * BLK * BLK
    return pl.pallas_call(
        functools.partial(spread_kernel, n, chunks, per_chunk, which),
        grid=(per_chunk,),
        in_specs=[smem()] * 2 + [h_spec] * chunks + [tile] * (chunks * n),
        out_specs=whole((count, width)),
        out_shape=jax.ShapeDtypeStruct((count, width), jnp.bfloat16),
        scratch_shapes=[pltpu.VMEM((count, width), jnp.float32)],
        compiler_params=params(),
        cost_estimate=pl.CostEstimate(flops=flops, bytes_accessed=14 * MIB, transcendentals=0),
        name="spread",
    )(me, index, *hs, *[w for chunk in ws for w in chunk])


def exchange(a, bit, n):
    return lax.ppermute(a, "fsdp", [(i, i ^ bit) for i in range(n)])


def gather(a, n, bits):
    held = {0: a}
    for bit in bits:
        for r in list(held):
            held[r ^ bit] = exchange(held[r], bit, n)
    return [held[r] for r in range(n)]


def body(n, tokens, out_grad, up_weight, down_weight, up_index, down_index):
    width = tokens.shape[1]
    slots = up_weight.shape[1]
    chunks = CHUNKS
    per_chunk = up_weight.shape[0] // chunks
    bits = [1 << b for b in range(n.bit_length() - 1)]
    me = lax.axis_index("fsdp").astype(jnp.int32).reshape(1)

    both = jnp.concatenate([tokens, out_grad], axis=1)
    mine = lax.all_gather(both, "tensor", axis=0, tiled=True)
    other = lax.all_gather(exchange(both, 1, n), "tensor", axis=0, tiled=True)

    ups, downs, hs, ups_grad, downs_grad = [], [], [], [], []
    for c in range(chunks):
        part = slice(c * per_chunk, (c + 1) * per_chunk)
        ups.append(gather(up_weight[part], n, bits))
        downs.append(gather(down_weight[part], n, bits[::-1]))
        hs.append(forward(n, c * per_chunk, me, up_index, down_index, mine, ups[c], downs[c]))

    mixed = spread(n, 0, me, down_index, hs, downs, width)
    mixed_rows = lax.psum_scatter(mixed, "tensor", scatter_dimension=0, tiled=True)
    spread_in = spread(n, 1, me, up_index, hs, ups, width)
    input_rows = lax.psum_scatter(spread_in, "tensor", scatter_dimension=0, tiled=True)

    for c in range(chunks):
        h_other = exchange(hs[c], 1, n)
        up, down, *sent = grads(
            n, c * per_chunk, me, up_index, down_index, mine, other, hs[c], h_other, slots
        )
        for e, part in enumerate(sent):
            got = exchange(part, 2 * (e + 1), n).astype(jnp.float32)
            up, down = up + got[0], down + got[1]
        ups_grad.append(up)
        downs_grad.append(down)
    up_grad = jnp.concatenate(ups_grad, axis=0)
    down_grad = jnp.concatenate(downs_grad, axis=0)
    return (mixed_rows, input_rows, up_grad, down_grad)


def solution(mesh):
    return jax.shard_map(
        functools.partial(body, mesh.shape["fsdp"]),
        mesh=mesh,
        in_specs=(
            P(("fsdp", "tensor"), None),
            P(("fsdp", "tensor"), None),
            P("tensor", "fsdp", None, None),
            P("tensor", "fsdp", None, None),
            P("tensor", None),
            P("tensor", None),
        ),
        out_specs=(
            P(("fsdp", "tensor"), None),
            P(("fsdp", "tensor"), None),
            P("tensor", "fsdp", None, None),
            P("tensor", "fsdp", None, None),
        ),
        check_vma=False,
    )
```

profile of v0, /device:TPU:0, one launch (start us, length us, event | category | flops | bytes accessed | tf_op | source)
XLA Modules:
  0.0 346.7 jit_solution(8554322732546714558)
XLA Ops:
  10.2 3.0 collective-permute-start.24
  13.2 17.8 %collective-permute-done.24 = bf16[24,16384]{1,0:T(8,128)(2,1)S(1)} collective-permute-done((bf16[24,16384]{1,0:T(8,128)(2,1)}, bf16[24,16384]{1,0:T(8,128)(2,1)S(1)}, u32[]{:S(2)}, u32[]{:S(2)}) %collective-permute-start.24) | collective-permute-done | bytes 786464 | tf_op jit(solution)/shard_map/ppermute | solution.py:178
  32.0 1.8 fusion.9
  33.8 1.8 collective-permute-start
  40.8 7.9 %collective-permute-done.refs_1_.refs_5_ = bf16[8,2,128,128]{3,2,1,0:T(8,128)(2,1)S(1)} collective-permute-done((bf16[8,2,128,128]{3,2,1,0:T(8,128)(2,1)S(1)}, bf16[8,2,128,128]{3,2,1,0:T(8,128)(2,1)S(1)}, u32[]{:S(2)}, u32[]{:S(2)}) %collective-permute-start) | collective-permute-done | bytes 524320 | tf_op jit(solution)/shard_map/ppermute | solution.py:178
  52.8 7.2 %collective-permute-done.3.refs_5_ = bf16[8,2,128,128]{3,2,1,0:T(8,128)(2,1)S(1)} collective-permute-done((bf16[8,2,128,128]{3,2,1,0:T(8,128)(2,1)S(1)}, bf16[8,2,128,128]{3,2,1,0:T(8,128)(2,1)S(1)}, u32[]{:S(2)}, u32[]{:S(2)}) %collective-permute-start.3) | collective-permute-done | bytes 524320 | tf_op jit(solution)/shard_map/ppermute | solution.py:178
  64.0 7.2 %collective-permute-done.6.refs_1_.refs_9_ = bf16[8,2,128,128]{3,2,1,0:T(8,128)(2,1)S(1)} collective-permute-done((bf16[8,2,128,128]{3,2,1,0:T(8,128)(2,1)S(1)}, bf16[8,2,128,128]{3,2,1,0:T(8,128)(2,1)S(1)}, u32[]{:S(2)}, u32[]{:S(2)}) %collective-permute-start.6) | collective-permute-done | bytes 524320 | tf_op jit(solution)/shard_map/ppermute | solution.py:178
  75.3 7.2 %collective-permute-done.9.refs_5_.refs_9_ = bf16[8,2,128,128]{3,2,1,0:T(8,128)(2,1)S(1)} collective-permute-done((bf16[8,2,128,128]{3,2,1,0:T(8,128)(2,1)S(1)}, bf16[8,2,128,128]{3,2,1,0:T(8,128)(2,1)S(1)}, u32[]{:S(2)}, u32[]{:S(2)}) %collective-permute-start.9) | collective-permute-done | bytes 524320 | tf_op jit(solution)/shard_map/ppermute | solution.py:178
  87.3 6.4 %collective-permute-done.12.refs_1_.refs_13_ = bf16[8,2,128,128]{3,2,1,0:T(8,128)(2,1)S(1)} collective-permute-done((bf16[8,2,128,128]{3,2,1,0:T(8,128)(2,1)S(1)}, bf16[8,2,128,128]{3,2,1,0:T(8,128)(2,1)S(1)}, u32[]{:S(2)}, u32[]{:S(2)}) %collective-permute-start.12) | collective-permute-done | bytes 524320 | tf_op jit(solution)/shard_map/ppermute | solution.py:178
  98.6 6.4 %collective-permute-done.15.refs_5_.refs_13_ = bf16[8,2,128,128]{3,2,1,0:T(8,128)(2,1)S(1)} collective-permute-done((bf16[8,2,128,128]{3,2,1,0:T(8,128)(2,1)S(1)}, bf16[8,2,128,128]{3,2,1,0:T(8,128)(2,1)S(1)}, u32[]{:S(2)}, u32[]{:S(2)}) %collective-permute-start.15) | collective-permute-done | bytes 524320 | tf_op jit(solution)/shard_map/ppermute | solution.py:178
  110.6 5.7 %collective-permute-done.18.refs_1_.refs_17_ = bf16[8,2,128,128]{3,2,1,0:T(8,128)(2,1)} collective-permute-done((bf16[8,2,128,128]{3,2,1,0:T(8,128)(2,1)S(1)}, bf16[8,2,128,128]{3,2,1,0:T(8,128)(2,1)}, u32[]{:S(2)}, u32[]{:S(2)}) %collective-permute-start.18) | collective-permute-done | bytes 524320 | tf_op jit(solution)/shard_map/ppermute | solution.py:178
  121.1 8.0 %collective-permute-done.2.refs_3_.refs_7_ = bf16[8,2,128,128]{3,2,1,0:T(8,128)(2,1)S(1)} collective-permute-done((bf16[8,2,128,128]{3,2,1,0:T(8,128)(2,1)S(1)}, bf16[8,2,128,128]{3,2,1,0:T(8,128)(2,1)S(1)}, u32[]{:S(2)}, u32[]{:S(2)}) %collective-permute-start.2) | collective-permute-done | bytes 524320 | tf_op jit(solution)/shard_map/ppermute | solution.py:178
  132.8 7.5 %collective-permute-done.8.refs_3_.refs_11_ = bf16[8,2,128,128]{3,2,1,0:T(8,128)(2,1)S(1)} collective-permute-done((bf16[8,2,128,128]{3,2,1,0:T(8,128)(2,1)S(1)}, bf16[8,2,128,128]{3,2,1,0:T(8,128)(2,1)S(1)}, u32[]{:S(2)}, u32[]{:S(2)}) %collective-permute-start.8) | collective-permute-done | bytes 524320 | tf_op jit(solution)/shard_map/ppermute | solution.py:178
  144.0 7.6 %collective-permute-done.14.refs_3_.refs_15_ = bf16[8,2,128,128]{3,2,1,0:T(8,128)(2,1)S(1)} collective-permute-done((bf16[8,2,128,128]{3,2,1,0:T(8,128)(2,1)S(1)}, bf16[8,2,128,128]{3,2,1,0:T(8,128)(2,1)S(1)}, u32[]{:S(2)}, u32[]{:S(2)}) %collective-permute-start.14) | collective-permute-done | bytes 524320 | tf_op jit(solution)/shard_map/ppermute | solution.py:178
  160.2 5.6 %forward_chunk.4.refs_0_.h_mine = bf16[2,8,192,128]{3,2,1,0:T(8,128)(2,1)S(1)} custom-call(s32[1]{0:T(128)} %bitcast.me_ref, s32[32,8]{1,0:T(8,128)S(1)} %copy.10.up_idx.idx, s32[32,8]{1,0:T(8,128)S(1)} %copy.18.down_idx.idx, bf16[192,16384]{1,0:T(8,128)(2,1)} %all-gather.3.cloned.1.call-done.rows_ref.mine, ...), custom_call_target="tpu_custom_call" | custom-call | flops 805306368 | bytes 10485760 | tf_op jit(solution)/shard_map/forward_chunk/pallas_call | solution.py:124
  166.8 5.6 %forward_chunk.5.refs_1_.h_mine = bf16[2,8,192,128]{3,2,1,0:T(8,128)(2,1)S(1)} custom-call(s32[1]{0:T(128)} %bitcast.me_ref, s32[32,8]{1,0:T(8,128)S(1)} %copy.10.up_idx.idx, s32[32,8]{1,0:T(8,128)S(1)} %copy.18.down_idx.idx, bf16[192,16384]{1,0:T(8,128)(2,1)} %all-gather.3.cloned.1.call-done.rows_ref.mine, ...), custom_call_target="tpu_custom_call" | custom-call | flops 805306368 | bytes 10485760 | tf_op jit(solution)/shard_map/forward_chunk/pallas_call | solution.py:124
  173.4 6.0 %forward_chunk.6.refs_2_.h_mine = bf16[2,8,192,128]{3,2,1,0:T(8,128)(2,1)S(1)} custom-call(s32[1]{0:T(128)} %bitcast.me_ref, s32[32,8]{1,0:T(8,128)S(1)} %copy.10.up_idx.idx, s32[32,8]{1,0:T(8,128)S(1)} %copy.18.down_idx.idx, bf16[192,16384]{1,0:T(8,128)(2,1)} %all-gather.3.cloned.1.call-done.rows_ref.mine, ...), custom_call_target="tpu_custom_call" | custom-call | flops 805306368 | bytes 10485760 | tf_op jit(solution)/shard_map/forward_chunk/pallas_call | solution.py:124
  180.3 6.6 %forward_chunk.7.refs_3_.h_mine = bf16[2,8,192,128]{3,2,1,0:T(8,128)(2,1)S(1)} custom-call(s32[1]{0:T(128)} %bitcast.me_ref, s32[32,8]{1,0:T(8,128)S(1)} %copy.10.up_idx.idx, s32[32,8]{1,0:T(8,128)S(1)} %copy.18.down_idx.idx, bf16[192,16384]{1,0:T(8,128)(2,1)} %all-gather.3.cloned.1.call-done.rows_ref.mine, ...), custom_call_target="tpu_custom_call" | custom-call | flops 805306368 | bytes 10485760 | tf_op jit(solution)/shard_map/forward_chunk/pallas_call | solution.py:124
  187.8 11.9 %spread.2 = bf16[192,8192]{1,0:T(8,128)(2,1)} custom-call(s32[1]{0:T(128)} %bitcast.me_ref, s32[32,8]{1,0:T(8,128)S(1)} %copy.18.down_idx.idx, bf16[2,8,192,128]{3,2,1,0:T(8,128)(2,1)} %copy-done, bf16[2,8,192,128]{3,2,1,0:T(8,128)(2,1)} %copy-done.2, bf16[2,8,192,128]{3,2,1,0:T(8,128)(2,1)} %copy-done.4, bf16[2,8,192,128]{3,2,1,0:T(8,128)(2,1)} %copy-done.6, ...), custom_call_target="tpu_custom_call" | custom-call | flops 1610612736 | bytes 14680064 | tf_op jit(solution)/shard_map/spread/pallas_call | solution.py:164
  211.7 11.8 %spread.3 = bf16[192,8192]{1,0:T(8,128)(2,1)} custom-call(s32[1]{0:T(128)} %bitcast.me_ref, s32[32,8]{1,0:T(8,128)S(1)} %copy.10.up_idx.idx, bf16[2,8,192,128]{3,2,1,0:T(8,128)(2,1)} %copy-done, bf16[2,8,192,128]{3,2,1,0:T(8,128)(2,1)} %copy-done.2, bf16[2,8,192,128]{3,2,1,0:T(8,128)(2,1)} %copy-done.4, bf16[2,8,192,128]{3,2,1,0:T(8,128)(2,1)} %copy-done.6, ...), custom_call_target="tpu_custom_call" | custom-call | flops 1610612736 | bytes 14680064 | tf_op jit(solution)/shard_map/spread/pallas_call | solution.py:164
  227.7 16.5 %collective-permute-done.31.h_other = bf16[2,8,192,128]{3,2,1,0:T(8,128)(2,1)} collective-permute-done((bf16[2,8,192,128]{3,2,1,0:T(8,128)(2,1)S(1)}, bf16[2,8,192,128]{3,2,1,0:T(8,128)(2,1)}, u32[]{:S(2)}, u32[]{:S(2)}) %collective-permute-start.31) | collective-permute-done | bytes 786464 | tf_op jit(solution)/shard_map/ppermute | solution.py:178
  244.2 7.9 %grad_chunk.7 = (f32[8,2,128,128]{3,2,1,0:T(8,128)S(1)}, f32[8,2,128,128]{3,2,1,0:T(8,128)S(1)}, bf16[2,8,2,128,128]{4,3,2,1,0:T(8,128)(2,1)S(1)}) custom-call(s32[1]{0:T(128)} %bitcast.me_ref, s32[32,8]{1,0:T(8,128)S(1)} %copy.10.up_idx.idx, s32[32,8]{1,0:T(8,128)S(1)} %copy.18.down_idx.idx, bf16[192,16384]{1,0:T(8,128)(2,1)} %all-gather.3.cloned.1.call-done.rows_ref.mine, ...), custom_call_target="tpu_custom_call" | custom-call | flops 805306368 | bytes 18874368 | tf_op jit(solution)/shard_map/grad_chunk/pallas_call | solution.py:145
  253.9 7.2 %collective-permute-done.29.h_other = bf16[2,8,192,128]{3,2,1,0:T(8,128)(2,1)} collective-permute-done((bf16[2,8,192,128]{3,2,1,0:T(8,128)(2,1)S(1)}, bf16[2,8,192,128]{3,2,1,0:T(8,128)(2,1)}, u32[]{:S(2)}, u32[]{:S(2)}) %collective-permute-start.29) | collective-permute-done | bytes 786464 | tf_op jit(solution)/shard_map/ppermute | solution.py:178
  261.0 8.0 %grad_chunk.6 = (f32[8,2,128,128]{3,2,1,0:T(8,128)S(1)}, f32[8,2,128,128]{3,2,1,0:T(8,128)S(1)}, bf16[2,8,2,128,128]{4,3,2,1,0:T(8,128)(2,1)S(1)}) custom-call(s32[1]{0:T(128)} %bitcast.me_ref, s32[32,8]{1,0:T(8,128)S(1)} %copy.10.up_idx.idx, s32[32,8]{1,0:T(8,128)S(1)} %copy.18.down_idx.idx, bf16[192,16384]{1,0:T(8,128)(2,1)} %all-gather.3.cloned.1.call-done.rows_ref.mine, ...), custom_call_target="tpu_custom_call" | custom-call | flops 805306368 | bytes 18874368 | tf_op jit(solution)/shard_map/grad_chunk/pallas_call | solution.py:145
  270.9 7.0 %collective-permute-done.27.h_other = bf16[2,8,192,128]{3,2,1,0:T(8,128)(2,1)} collective-permute-done((bf16[2,8,192,128]{3,2,1,0:T(8,128)(2,1)S(1)}, bf16[2,8,192,128]{3,2,1,0:T(8,128)(2,1)}, u32[]{:S(2)}, u32[]{:S(2)}) %collective-permute-start.27) | collective-permute-done | bytes 786464 | tf_op jit(solution)/shard_map/ppermute | solution.py:178
  277.9 8.0 %grad_chunk.5 = (f32[8,2,128,128]{3,2,1,0:T(8,128)S(1)}, f32[8,2,128,128]{3,2,1,0:T(8,128)S(1)}, bf16[2,8,2,128,128]{4,3,2,1,0:T(8,128)(2,1)S(1)}) custom-call(s32[1]{0:T(128)} %bitcast.me_ref, s32[32,8]{1,0:T(8,128)S(1)} %copy.10.up_idx.idx, s32[32,8]{1,0:T(8,128)S(1)} %copy.18.down_idx.idx, bf16[192,16384]{1,0:T(8,128)(2,1)} %all-gather.3.cloned.1.call-done.rows_ref.mine, ...), custom_call_target="tpu_custom_call" | custom-call | flops 805306368 | bytes 18874368 | tf_op jit(solution)/shard_map/grad_chunk/pallas_call | solution.py:145
  285.9 1.8 collective-permute-start.28
  287.7 2.0 collective-permute-done.25.h_other
  289.7 7.9 %grad_chunk.4 = (f32[8,2,128,128]{3,2,1,0:T(8,128)S(1)}, f32[8,2,128,128]{3,2,1,0:T(8,128)S(1)}, bf16[2,8,2,128,128]{4,3,2,1,0:T(8,128)(2,1)S(1)}) custom-call(s32[1]{0:T(128)} %bitcast.me_ref, s32[32,8]{1,0:T(8,128)S(1)} %copy.10.up_idx.idx, s32[32,8]{1,0:T(8,128)S(1)} %copy.18.down_idx.idx, bf16[192,16384]{1,0:T(8,128)(2,1)} %all-gather.3.cloned.1.call-done.rows_ref.mine, ...), custom_call_target="tpu_custom_call" | custom-call | flops 805306368 | bytes 18874368 | tf_op jit(solution)/shard_map/grad_chunk/pallas_call | solution.py:145
  301.8 16.2 %collective-permute-done.28 = bf16[2,8,2,128,128]{4,3,2,1,0:T(8,128)(2,1)} collective-permute-done((bf16[2,8,2,128,128]{4,3,2,1,0:T(8,128)(2,1)S(1)}, bf16[2,8,2,128,128]{4,3,2,1,0:T(8,128)(2,1)}, u32[]{:S(2)}, u32[]{:S(2)}) %collective-permute-start.28) | collective-permute-done | bytes 1048608 | tf_op jit(solution)/shard_map/ppermute | solution.py:178
  319.5 15.3 %collective-permute-done.26 = bf16[2,8,2,128,128]{4,3,2,1,0:T(8,128)(2,1)S(1)} collective-permute-done((bf16[2,8,2,128,128]{4,3,2,1,0:T(8,128)(2,1)S(1)}, bf16[2,8,2,128,128]{4,3,2,1,0:T(8,128)(2,1)S(1)}, u32[]{:S(2)}, u32[]{:S(2)}) %collective-permute-start.26) | collective-permute-done | bytes 1048608 | tf_op jit(solution)/shard_map/ppermute | solution.py:178
  336.4 3.8 %pad_maximum_fusion = (f32[32,2,128,128]{3,2,1,0:T(8,128)}, f32[32,2,128,128]{3,2,1,0:T(8,128)}) fusion(f32[8,2,128,128]{3,2,1,0:T(8,128)S(1)} %get-tuple-element.35, f32[8,2,128,128]{3,2,1,0:T(8,128)S(1)} %get-tuple-element.33, f32[8,2,128,128]{3,2,1,0:T(8,128)S(1)} %get-tuple-element.31, f32[8,2,128,128]{3,2,1,0:T(8,128)S(1)} %get-tuple-element.29, ...), kind=kLoop, calls=%fused_computation | loop fusion | flops 6291456 | bytes 16777216 | tf_op jit(solution)/shard_map/concatenate | solution.py:223
  (209 shorter events, 87.8 us)
Async XLA Ops:
  7.2 145.7 %all-gather.3.cloned.1.call-start = ((), (), s32[]{:S(2)}) async-start(), calls=%async_computation.2 | async-start | bytes 7077888 | tf_op jit(solution)/shard_map/all_gather | solution.py:198
  10.2 217.5 %all-gather.5.cloned.1.call-start = ((), (), s32[]{:S(2)}) async-start(), calls=%async_computation.5 | async-start | bytes 7077888 | tf_op jit(solution)/shard_map/all_gather | solution.py:199
  31.9 308.3 %reduce-scatter.3.cloned.1.call-start = ((), (), s32[]{:S(2)}) async-start(), calls=%async_computation.3 | async-start | bytes 3538944 | tf_op jit(solution)/shard_map/reduce_scatter | solution.py:209
  38.0 24.6 %collective-permute-start.4 = (bf16[8,2,128,128]{3,2,1,0:T(8,128)(2,1)S(1)}, bf16[8,2,128,128]{3,2,1,0:T(8,128)(2,1)S(1)}, u32[]{:S(2)}, u32[]{:S(2)}) collective-permute-start(bf16[8,2,128,128]{3,2,1,0:T(8,128)(2,1)S(1)} %get-tuple-element.38.refs_4_), channel_id=1, source_target_pairs={{0,16},{8,24},{16,0},{24,8},{1,17},{9,25},{17,1},{25,9},{2,18},{10... | collective-permute-start | bytes 1572872 | tf_op jit(solution)/shard_map/ppermute | solution.py:178
  39.1 32.1 %collective-permute-start.6 = (bf16[8,2,128,128]{3,2,1,0:T(8,128)(2,1)S(1)}, bf16[8,2,128,128]{3,2,1,0:T(8,128)(2,1)S(1)}, u32[]{:S(2)}, u32[]{:S(2)}) collective-permute-start(bf16[8,2,128,128]{3,2,1,0:T(8,128)(2,1)S(1)} %get-tuple-element.41.refs_0_.refs_8_), channel_id=1, source_target_pairs={{0,8},{8,0},{16,24},{24,16},{1,9},{9,1},{17,25},{25,17},{2,10},{10... | collective-permute-start | bytes 1572872 | tf_op jit(solution)/shard_map/ppermute | solution.py:178
  48.8 24.2 %collective-permute-start.7 = (bf16[8,2,128,128]{3,2,1,0:T(8,128)(2,1)S(1)}, bf16[8,2,128,128]{3,2,1,0:T(8,128)(2,1)S(1)}, u32[]{:S(2)}, u32[]{:S(2)}) collective-permute-start(bf16[8,2,128,128]{3,2,1,0:T(8,128)(2,1)S(1)} %get-tuple-element.41.refs_0_.refs_8_), channel_id=1, source_target_pairs={{0,16},{8,24},{16,0},{24,8},{1,17},{9,25},{17,1},{25,9},{2,18},{10... | collective-permute-start | bytes 1572872 | tf_op jit(solution)/shard_map/ppermute | solution.py:178
  51.3 31.1 %collective-permute-start.9 = (bf16[8,2,128,128]{3,2,1,0:T(8,128)(2,1)S(1)}, bf16[8,2,128,128]{3,2,1,0:T(8,128)(2,1)S(1)}, u32[]{:S(2)}, u32[]{:S(2)}) collective-permute-start(bf16[8,2,128,128]{3,2,1,0:T(8,128)(2,1)S(1)} %get-tuple-element.37.refs_4_.refs_8_), channel_id=1, source_target_pairs={{0,8},{8,0},{16,24},{24,16},{1,9},{9,1},{17,25},{25,17},{2,10},{10... | collective-permute-start | bytes 1572872 | tf_op jit(solution)/shard_map/ppermute | solution.py:178
  60.8 25.0 %collective-permute-start.10 = (bf16[8,2,128,128]{3,2,1,0:T(8,128)(2,1)S(1)}, bf16[8,2,128,128]{3,2,1,0:T(8,128)(2,1)S(1)}, u32[]{:S(2)}, u32[]{:S(2)}) collective-permute-start(bf16[8,2,128,128]{3,2,1,0:T(8,128)(2,1)S(1)} %get-tuple-element.37.refs_4_.refs_8_), channel_id=1, source_target_pairs={{0,16},{8,24},{16,0},{24,8},{1,17},{9,25},{17,1},{25,9},{2,18},{10... | collective-permute-start | bytes 1572872 | tf_op jit(solution)/shard_map/ppermute | solution.py:178
  62.5 31.1 %collective-permute-start.12 = (bf16[8,2,128,128]{3,2,1,0:T(8,128)(2,1)S(1)}, bf16[8,2,128,128]{3,2,1,0:T(8,128)(2,1)S(1)}, u32[]{:S(2)}, u32[]{:S(2)}) collective-permute-start(bf16[8,2,128,128]{3,2,1,0:T(8,128)(2,1)S(1)} %get-tuple-element.43.refs_0_.refs_12_), channel_id=1, source_target_pairs={{0,8},{8,0},{16,24},{24,16},{1,9},{9,1},{17,25},{25,17},{2,10},{10... | collective-permute-start | bytes 1572872 | tf_op jit(solution)/shard_map/ppermute | solution.py:178
  71.2 24.2 %collective-permute-start.13 = (bf16[8,2,128,128]{3,2,1,0:T(8,128)(2,1)S(1)}, bf16[8,2,128,128]{3,2,1,0:T(8,128)(2,1)S(1)}, u32[]{:S(2)}, u32[]{:S(2)}) collective-permute-start(bf16[8,2,128,128]{3,2,1,0:T(8,128)(2,1)S(1)} %get-tuple-element.43.refs_0_.refs_12_), channel_id=1, source_target_pairs={{0,16},{8,24},{16,0},{24,8},{1,17},{9,25},{17,1},{25,9},{2,18},{10... | collective-permute-start | bytes 1572872 | tf_op jit(solution)/shard_map/ppermute | solution.py:178
  73.8 31.1 %collective-permute-start.15 = (bf16[8,2,128,128]{3,2,1,0:T(8,128)(2,1)S(1)}, bf16[8,2,128,128]{3,2,1,0:T(8,128)(2,1)S(1)}, u32[]{:S(2)}, u32[]{:S(2)}) collective-permute-start(bf16[8,2,128,128]{3,2,1,0:T(8,128)(2,1)S(1)} %get-tuple-element.39.refs_4_.refs_12_), channel_id=1, source_target_pairs={{0,8},{8,0},{16,24},{24,16},{1,9},{9,1},{17,25},{25,17},{2,10},{10... | collective-permute-start | bytes 1572872 | tf_op jit(solution)/shard_map/ppermute | solution.py:178
  83.3 25.0 %collective-permute-start.16 = (bf16[8,2,128,128]{3,2,1,0:T(8,128)(2,1)S(1)}, bf16[8,2,128,128]{3,2,1,0:T(8,128)(2,1)}, u32[]{:S(2)}, u32[]{:S(2)}) collective-permute-start(bf16[8,2,128,128]{3,2,1,0:T(8,128)(2,1)S(1)} %get-tuple-element.39.refs_4_.refs_12_), channel_id=1, source_target_pairs={{0,16},{8,24},{16,0},{24,8},{1,17},{9,25},{17,1},{25,9},{2,18},{10... | collective-permute-start | bytes 1572872 | tf_op jit(solution)/shard_map/ppermute | solution.py:178
  85.8 30.5 %collective-permute-start.18 = (bf16[8,2,128,128]{3,2,1,0:T(8,128)(2,1)S(1)}, bf16[8,2,128,128]{3,2,1,0:T(8,128)(2,1)}, u32[]{:S(2)}, u32[]{:S(2)}) collective-permute-start(bf16[8,2,128,128]{3,2,1,0:T(8,128)(2,1)S(1)} %get-tuple-element.40.refs_0_.refs_16_), channel_id=1, source_target_pairs={{0,8},{8,0},{16,24},{24,16},{1,9},{9,1},{17,25},{25,17},{2,10},{10... | collective-permute-start | bytes 1572872 | tf_op jit(solution)/shard_map/ppermute | solution.py:178
  93.7 25.1 %collective-permute-start.22 = (bf16[8,2,128,128]{3,2,1,0:T(8,128)(2,1)S(1)}, bf16[8,2,128,128]{3,2,1,0:T(8,128)(2,1)}, u32[]{:S(2)}, u32[]{:S(2)}) collective-permute-start(bf16[8,2,128,128]{3,2,1,0:T(8,128)(2,1)S(1)} %get-tuple-element.36.refs_4_.refs_16_), channel_id=1, source_target_pairs={{0,16},{8,24},{16,0},{24,8},{1,17},{9,25},{17,1},{25,9},{2,18},{10... | collective-permute-start | bytes 1572872 | tf_op jit(solution)/shard_map/ppermute | solution.py:178
  96.2 32.9 %collective-permute-start.2 = (bf16[8,2,128,128]{3,2,1,0:T(8,128)(2,1)S(1)}, bf16[8,2,128,128]{3,2,1,0:T(8,128)(2,1)S(1)}, u32[]{:S(2)}, u32[]{:S(2)}) collective-permute-start(bf16[8,2,128,128]{3,2,1,0:T(8,128)(2,1)S(1)} %collective-permute-done.refs_1_.refs_5_), channel_id=1, source_target_pairs={{0,16},{8,24},{16,0},{24,8},{1,17},{9,25},{17,1},{25,9},{2,18},{10... | collective-permute-start | bytes 1572872 | tf_op jit(solution)/shard_map/ppermute | solution.py:178
  105.7 24.5 %collective-permute-start.5 = (bf16[8,2,128,128]{3,2,1,0:T(8,128)(2,1)S(1)}, bf16[8,2,128,128]{3,2,1,0:T(8,128)(2,1)S(1)}, u32[]{:S(2)}, u32[]{:S(2)}) collective-permute-start(bf16[8,2,128,128]{3,2,1,0:T(8,128)(2,1)S(1)} %collective-permute-done.4.refs_6_), channel_id=1, source_target_pairs={{0,8},{8,0},{16,24},{24,16},{1,9},{9,1},{17,25},{25,17},{2,10},{10... | collective-permute-start | bytes 1572872 | tf_op jit(solution)/shard_map/ppermute | solution.py:178
  108.3 32.1 %collective-permute-start.8 = (bf16[8,2,128,128]{3,2,1,0:T(8,128)(2,1)S(1)}, bf16[8,2,128,128]{3,2,1,0:T(8,128)(2,1)S(1)}, u32[]{:S(2)}, u32[]{:S(2)}) collective-permute-start(bf16[8,2,128,128]{3,2,1,0:T(8,128)(2,1)S(1)} %collective-permute-done.6.refs_1_.refs_9_), channel_id=1, source_target_pairs={{0,16},{8,24},{16,0},{24,8},{1,17},{9,25},{17,1},{25,9},{2,18},{10... | collective-permute-start | bytes 1572872 | tf_op jit(solution)/shard_map/ppermute | solution.py:178
  116.3 25.2 %collective-permute-start.11 = (bf16[8,2,128,128]{3,2,1,0:T(8,128)(2,1)S(1)}, bf16[8,2,128,128]{3,2,1,0:T(8,128)(2,1)S(1)}, u32[]{:S(2)}, u32[]{:S(2)}) collective-permute-start(bf16[8,2,128,128]{3,2,1,0:T(8,128)(2,1)S(1)} %collective-permute-done.10.refs_6_.refs_10_), channel_id=1, source_target_pairs={{0,8},{8,0},{16,24},{24,16},{1,9},{9,1},{17,25},{25,17},{2,10},{10... | collective-permute-start | bytes 1572872 | tf_op jit(solution)/shard_map/ppermute | solution.py:178
  118.8 32.8 %collective-permute-start.14 = (bf16[8,2,128,128]{3,2,1,0:T(8,128)(2,1)S(1)}, bf16[8,2,128,128]{3,2,1,0:T(8,128)(2,1)S(1)}, u32[]{:S(2)}, u32[]{:S(2)}) collective-permute-start(bf16[8,2,128,128]{3,2,1,0:T(8,128)(2,1)S(1)} %collective-permute-done.12.refs_1_.refs_13_), channel_id=1, source_target_pairs={{0,16},{8,24},{16,0},{24,8},{1,17},{9,25},{17,1},{25,9},{2,18},{10... | collective-permute-start | bytes 1572872 | tf_op jit(solution)/shard_map/ppermute | solution.py:178
  130.0 43.4 %collective-permute-start.17 = (bf16[8,2,128,128]{3,2,1,0:T(8,128)(2,1)}, bf16[8,2,128,128]{3,2,1,0:T(8,128)(2,1)}, u32[]{:S(2)}, u32[]{:S(2)}) collective-permute-start(bf16[8,2,128,128]{3,2,1,0:T(8,128)(2,1)} %collective-permute-done.16.refs_6_.refs_14_), channel_id=1, source_target_pairs={{0,8},{8,0},{16,24},{24,16},{1,9},{9,1},{17,25},{25,17},{2,10},{10... | collective-permute-start | bytes 1572872 | tf_op jit(solution)/shard_map/ppermute | solution.py:178
  131.1 49.2 %collective-permute-start.19 = (bf16[8,2,128,128]{3,2,1,0:T(8,128)(2,1)S(1)}, bf16[8,2,128,128]{3,2,1,0:T(8,128)(2,1)}, u32[]{:S(2)}, u32[]{:S(2)}) collective-permute-start(bf16[8,2,128,128]{3,2,1,0:T(8,128)(2,1)S(1)} %get-tuple-element.40.refs_0_.refs_16_), channel_id=1, source_target_pairs={{0,16},{8,24},{16,0},{24,8},{1,17},{9,25},{17,1},{25,9},{2,18},{10... | collective-permute-start | bytes 1572872 | tf_op jit(solution)/shard_map/ppermute | solution.py:178
  141.1 39.1 %collective-permute-start.21 = (bf16[8,2,128,128]{3,2,1,0:T(8,128)(2,1)S(1)}, bf16[8,2,128,128]{3,2,1,0:T(8,128)(2,1)}, u32[]{:S(2)}, u32[]{:S(2)}) collective-permute-start(bf16[8,2,128,128]{3,2,1,0:T(8,128)(2,1)S(1)} %get-tuple-element.36.refs_4_.refs_16_), channel_id=1, source_target_pairs={{0,8},{8,0},{16,24},{24,16},{1,9},{9,1},{17,25},{25,17},{2,10},{10... | collective-permute-start | bytes 1572872 | tf_op jit(solution)/shard_map/ppermute | solution.py:178
  142.3 38.0 %collective-permute-start.20 = (bf16[8,2,128,128]{3,2,1,0:T(8,128)(2,1)}, bf16[8,2,128,128]{3,2,1,0:T(8,128)(2,1)}, u32[]{:S(2)}, u32[]{:S(2)}) collective-permute-start(bf16[8,2,128,128]{3,2,1,0:T(8,128)(2,1)} %collective-permute-done.18.refs_1_.refs_17_), channel_id=1, source_target_pairs={{0,16},{8,24},{16,0},{24,8},{1,17},{9,25},{17,1},{25,9},{2,18},{10... | collective-permute-start | bytes 1572872 | tf_op jit(solution)/shard_map/ppermute | solution.py:178
  152.4 27.9 %collective-permute-start.23 = (bf16[8,2,128,128]{3,2,1,0:T(8,128)(2,1)}, bf16[8,2,128,128]{3,2,1,0:T(8,128)(2,1)}, u32[]{:S(2)}, u32[]{:S(2)}) collective-permute-start(bf16[8,2,128,128]{3,2,1,0:T(8,128)(2,1)} %collective-permute-done.22.refs_6_.refs_18_), channel_id=1, source_target_pairs={{0,8},{8,0},{16,24},{24,16},{1,9},{9,1},{17,25},{25,17},{2,10},{10... | collective-permute-start | bytes 1572872 | tf_op jit(solution)/shard_map/ppermute | solution.py:178
  199.8 140.4 %reduce-scatter.5.cloned.1.call-start = ((), (), s32[]{:S(2)}) async-start(), calls=%async_computation.4 | async-start | bytes 3538944 | tf_op jit(solution)/shard_map/reduce_scatter | solution.py:211
  225.3 35.8 %collective-permute-start.29 = (bf16[2,8,192,128]{3,2,1,0:T(8,128)(2,1)S(1)}, bf16[2,8,192,128]{3,2,1,0:T(8,128)(2,1)}, u32[]{:S(2)}, u32[]{:S(2)}) collective-permute-start(bf16[2,8,192,128]{3,2,1,0:T(8,128)(2,1)S(1)} %copy-done.5), channel_id=1, source_target_pairs={{0,8},{8,0},{16,24},{24,16},{1,9},{9,1},{17,25},{25,17},{2,10},{10... | collective-permute-start | bytes 2359304 | tf_op jit(solution)/shard_map/ppermute | solution.py:178
  225.6 52.3 %collective-permute-start.27 = (bf16[2,8,192,128]{3,2,1,0:T(8,128)(2,1)S(1)}, bf16[2,8,192,128]{3,2,1,0:T(8,128)(2,1)}, u32[]{:S(2)}, u32[]{:S(2)}) collective-permute-start(bf16[2,8,192,128]{3,2,1,0:T(8,128)(2,1)S(1)} %copy-done.3), channel_id=1, source_target_pairs={{0,8},{8,0},{16,24},{24,16},{1,9},{9,1},{17,25},{25,17},{2,10},{10... | collective-permute-start | bytes 2359304 | tf_op jit(solution)/shard_map/ppermute | solution.py:178
  227.3 62.4 %collective-permute-start.25 = (bf16[2,8,192,128]{3,2,1,0:T(8,128)(2,1)S(1)}, bf16[2,8,192,128]{3,2,1,0:T(8,128)(2,1)}, u32[]{:S(2)}, u32[]{:S(2)}) collective-permute-start(bf16[2,8,192,128]{3,2,1,0:T(8,128)(2,1)S(1)} %copy-done.1), channel_id=1, source_target_pairs={{0,8},{8,0},{16,24},{24,16},{1,9},{9,1},{17,25},{25,17},{2,10},{10... | collective-permute-start | bytes 2359304 | tf_op jit(solution)/shard_map/ppermute | solution.py:178
  252.1 46.8 %collective-permute-start.32 = (bf16[2,8,2,128,128]{4,3,2,1,0:T(8,128)(2,1)S(1)}, bf16[2,8,2,128,128]{4,3,2,1,0:T(8,128)(2,1)}, u32[]{:S(2)}, u32[]{:S(2)}) collective-permute-start(bf16[2,8,2,128,128]{4,3,2,1,0:T(8,128)(2,1)S(1)} %get-tuple-element.23), channel_id=1, source_target_pairs={{0,16},{8,24},{16,0},{24,8},{1,17},{9,25},{17,1},{25,9},{2,18},{10... | collective-permute-start | bytes 3145736 | tf_op jit(solution)/shard_map/ppermute | solution.py:178
  269.1 31.3 %collective-permute-start.30 = (bf16[2,8,2,128,128]{4,3,2,1,0:T(8,128)(2,1)S(1)}, bf16[2,8,2,128,128]{4,3,2,1,0:T(8,128)(2,1)}, u32[]{:S(2)}, u32[]{:S(2)}) collective-permute-start(bf16[2,8,2,128,128]{4,3,2,1,0:T(8,128)(2,1)S(1)} %get-tuple-element.21), channel_id=1, source_target_pairs={{0,16},{8,24},{16,0},{24,8},{1,17},{9,25},{17,1},{25,9},{2,18},{10... | collective-permute-start | bytes 3145736 | tf_op jit(solution)/shard_map/ppermute | solution.py:178
  285.9 32.1 %collective-permute-start.28 = (bf16[2,8,2,128,128]{4,3,2,1,0:T(8,128)(2,1)S(1)}, bf16[2,8,2,128,128]{4,3,2,1,0:T(8,128)(2,1)}, u32[]{:S(2)}, u32[]{:S(2)}) collective-permute-start(bf16[2,8,2,128,128]{4,3,2,1,0:T(8,128)(2,1)S(1)} %get-tuple-element.19), channel_id=1, source_target_pairs={{0,16},{8,24},{16,0},{24,8},{1,17},{9,25},{17,1},{25,9},{2,18},{10... | collective-permute-start | bytes 3145736 | tf_op jit(solution)/shard_map/ppermute | solution.py:178
  297.6 37.2 %collective-permute-start.26 = (bf16[2,8,2,128,128]{4,3,2,1,0:T(8,128)(2,1)S(1)}, bf16[2,8,2,128,128]{4,3,2,1,0:T(8,128)(2,1)S(1)}, u32[]{:S(2)}, u32[]{:S(2)}) collective-permute-start(bf16[2,8,2,128,128]{4,3,2,1,0:T(8,128)(2,1)S(1)} %get-tuple-element.17), channel_id=1, source_target_pairs={{0,16},{8,24},{16,0},{24,8},{1,17},{9,25},{17,1},{25,9},{2,18},{10... | collective-permute-start | bytes 3145736 | tf_op jit(solution)/shard_map/ppermute | solution.py:178
  (74 other events, 1277.5 us)
Sparse Core Ops, SparseCore 0:
  10.3 67.4 all-gather.2
  79.4 63.3 all-gather.4
  199.9 41.8 reduce-scatter.2
  244.5 39.4 reduce-scatter.4
where the time goes:
time: 349 us; the launch traced here: 347 us
  waiting for transfers between devices  153 us (44%)
  Pallas kernels  79.3 us (23%)
  starting transfers between devices  47.2 us (14%)
  local copies, waits for them, and re-layouts  43.1 us (12%)
  between operations  14.3 us (4%)
  other arithmetic  9.69 us (3%)
    ppermute x33, waiting for transfers between devices, exchange(): return lax.ppermute(a, 'fsdp', [(i, i ^ bit) for i in range(n)])  153 us
    ppermute x33, starting transfers between devices, exchange(): return lax.ppermute(a, 'fsdp', [(i, i ^ bit) for i in range(n)])  46.8 us
    unnamed x141, local copies, waits for them, and re-layouts  40 us
    pallas_call x4, Pallas kernels, grads(): pl.pallas_call(functools.partial(grad_kernel, n, first, per_step), grid=(...  31.8 us
    pallas_call x4, Pallas kernels, forward(): pl.pallas_call(functools.partial(forward_kernel, n, first, per_step), gri...  23.7 us
    pallas_call x2, Pallas kernels, spread(): pl.pallas_call(functools.partial(spread_kernel, n, chunks, per_chunk, whi...  23.7 us
  transfers between devices with their start and end apart: 37, of which 17 were waited for; matrix products, arithmetic and copies ran while one was open for 3% of the time, Pallas kernels for 23%

commit v1 on v0

v1 whole, which is shorter than its diff:
```python
import functools

import jax
import jax.numpy as jnp
from jax import lax
from jax.experimental import pallas as pl
from jax.experimental.pallas import tpu as pltpu
from jax.sharding import PartitionSpec as P

BLK = 128
CHUNKS = 4
MIB = 1 << 20
NT = (((1,), (1,)), ((), ()))
TN = (((0,), (0,)), ((), ()))


def dot(a, b, dims=(((1,), (0,)), ((), ()))):
    return lax.dot_general(a, b, dims, preferred_element_type=jnp.float32)


def columns(ref, blocks, offset=0):
    parts = [ref[:, pl.ds(pl.multiple_of(b * BLK + offset, BLK), BLK)] for b in blocks]
    return parts[0] if len(parts) == 1 else jnp.concatenate(parts, axis=1)


def side_by_side(ref, j, slots):
    parts = [ref[j, s] for s in range(slots)]
    return parts[0] if len(parts) == 1 else jnp.concatenate(parts, axis=1)


def hidden_pair(n, j, jj, me, up_idx, down_idx, rows, ups, downs):
    slots = ups[0].shape[1]
    width = rows.shape[1] // 2
    pre = jnp.zeros((rows.shape[0], BLK), jnp.float32)
    grad = jnp.zeros((rows.shape[0], BLK), jnp.float32)
    for r in range(n):
        k = (me ^ r) * slots
        chosen = columns(rows, [up_idx[j, k + s] for s in range(slots)])
        pre = pre + dot(chosen, ups[r][jj].reshape(slots * BLK, BLK))
        picked = columns(rows, [down_idx[j, k + s] for s in range(slots)], width)
        grad = grad + dot(picked, side_by_side(downs[r], jj, slots), NT)
    sigma = jax.nn.sigmoid(pre)
    hidden = (pre * sigma).astype(jnp.bfloat16)
    return hidden, (grad * sigma * (1.0 + pre * (1.0 - sigma))).astype(jnp.bfloat16)


def forward_kernel(n, first, per_step, me_ref, up_idx, down_idx, rows, *refs):
    ups, downs, out_ref = refs[:n], refs[n : 2 * n], refs[2 * n]
    for jj in range(per_step):
        j = first + pl.program_id(0) * per_step + jj
        hidden, pre_grad = hidden_pair(n, j, jj, me_ref[0], up_idx, down_idx, rows, ups, downs)
        out_ref[0, jj] = hidden
        out_ref[1, jj] = pre_grad


def grad_kernel(n, first, per_step, me_ref, up_idx, down_idx, mine, other, h_mine, *refs):
    ups, downs, outs = refs[:n], refs[n : 2 * n], refs[2 * n :]
    slots = outs[0].shape[1]
    width = mine.shape[1] // 2
    me = me_ref[0]
    for jj in range(per_step):
        j = first + pl.program_id(0) * per_step + jj
        hidden, pre_grad = hidden_pair(n, j, jj, me, up_idx, down_idx, other, ups, downs)
        for e, r in enumerate(range(0, n, 2)):
            k = (me ^ r) * slots
            up_cols = [up_idx[j, k + s] for s in range(slots)]
            down_cols = [down_idx[j, k + s] for s in range(slots)]
            up = dot(columns(mine, up_cols), h_mine[1, jj], TN)
            up = up + dot(columns(other, up_cols), pre_grad, TN)
            down = dot(h_mine[0, jj], columns(mine, down_cols, width), TN)
            down = down + dot(hidden, columns(other, down_cols, width), TN)
            for s in range(slots):
                up_tile = up[s * BLK : (s + 1) * BLK]
                down_tile = down[:, s * BLK : (s + 1) * BLK]
                if e == 0:
                    outs[0][jj, s] = up_tile
                    outs[1][jj, s] = down_tile
                else:
                    outs[1 + e][0, jj, s] = up_tile.astype(jnp.bfloat16)
                    outs[1 + e][1, jj, s] = down_tile.astype(jnp.bfloat16)


def spread_kernel(n, firsts, which, per_step, me_ref, idx, *refs):
    chunks = len(firsts)
    hs, ws = refs[:chunks], refs[chunks : chunks + chunks * n]
    out_ref, acc = refs[-2:]
    slots = ws[0].shape[1]
    me = me_ref[0]
    step = pl.program_id(0)

    @pl.when(step == 0)
    def _():
        @pl.loop(0, acc.shape[0] // 16)
        def _(i):
            acc[pl.ds(pl.multiple_of(i * 16, 16), 16)] = jnp.zeros((16, acc.shape[1]), acc.dtype)

    for c, first in enumerate(firsts):
        for jj in range(per_step):
            j = first + step * per_step + jj
            h = hs[c][0, jj]
            for r in range(n):
                k = (me ^ r) * slots
                w = ws[c * n + r]
                if which == 0:
                    terms = dot(h, side_by_side(w, jj, slots))
                else:
                    terms = dot(h, w[jj].reshape(slots * BLK, BLK), NT)
                for s in range(slots):
                    at = pl.ds(pl.multiple_of(idx[j, k + s] * BLK, BLK), BLK)
                    acc[:, at] += terms[:, s * BLK : (s + 1) * BLK]

    @pl.when(step == pl.num_programs(0) - 1)
    def _():
        @pl.loop(0, acc.shape[0] // 16)
        def _(i):
            at = pl.ds(pl.multiple_of(i * 16, 16), 16)
            out_ref[at] = acc[at].astype(out_ref.dtype)


def finish_kernel(count, own_up, own_down, *refs):
    up_ref, down_ref = refs[-2:]
    up, down = own_up[...], own_down[...]
    for got in refs[:count]:
        up = up + got[0].astype(jnp.float32)
        down = down + got[1].astype(jnp.float32)
    up_ref[...] = up
    down_ref[...] = down


def smem():
    return pl.BlockSpec(memory_space=pltpu.SMEM)


def whole(shape):
    return pl.BlockSpec(shape, lambda i: (0,) * len(shape), pipeline_mode=pl.Buffered(1))


def params():
    return pltpu.CompilerParams(vmem_limit_bytes=60 * MIB)


def forward(n, first, me, up_index, down_index, rows, ups, downs):
    per_chunk, slots = ups[0].shape[:2]
    count = rows.shape[0]
    per_step = 2
    tile = pl.BlockSpec((per_step, slots, BLK, BLK), lambda i: (i, 0, 0, 0))
    return pl.pallas_call(
        functools.partial(forward_kernel, n, first, per_step),
        grid=(per_chunk // per_step,),
        in_specs=[smem()] * 3 + [whole(rows.shape)] + [tile] * (2 * n),
        out_specs=pl.BlockSpec((2, per_step, count, BLK), lambda i: (0, i, 0, 0)),
        out_shape=jax.ShapeDtypeStruct((2, per_chunk, count, BLK), jnp.bfloat16),
        compiler_params=params(),
        cost_estimate=pl.CostEstimate(flops=0, bytes_accessed=MIB // 64, transcendentals=0),
        name="forward_chunk",
    )(me, up_index, down_index, rows, *ups, *downs)


def grads(n, first, me, up_index, down_index, mine, other, h_mine, ups, downs):
    per_chunk, slots = ups[0].shape[:2]
    count = h_mine.shape[2]
    per_step = 2
    h_spec = pl.BlockSpec((2, per_step, count, BLK), lambda i: (0, i, 0, 0))
    tile = pl.BlockSpec((per_step, slots, BLK, BLK), lambda i: (i, 0, 0, 0))
    sent = pl.BlockSpec((2, per_step, slots, BLK, BLK), lambda i: (0, i, 0, 0, 0))
    own_shape = jax.ShapeDtypeStruct((per_chunk, slots, BLK, BLK), jnp.float32)
    sent_shape = jax.ShapeDtypeStruct((2, per_chunk, slots, BLK, BLK), jnp.bfloat16)
    return pl.pallas_call(
        functools.partial(grad_kernel, n, first, per_step),
        grid=(per_chunk // per_step,),
        in_specs=[smem()] * 3 + [whole(mine.shape)] * 2 + [h_spec] + [tile] * (2 * n),
        out_specs=[tile] * 2 + [sent] * (n // 2 - 1),
        out_shape=[own_shape] * 2 + [sent_shape] * (n // 2 - 1),
        compiler_params=params(),
        cost_estimate=pl.CostEstimate(flops=0, bytes_accessed=MIB // 64, transcendentals=0),
        name="grad_chunk",
    )(me, up_index, down_index, mine, other, h_mine, *ups, *downs)


def spread(n, which, firsts, me, index, hs, ws, width):
    chunks = len(hs)
    per_chunk, count = hs[0].shape[1:3]
    slots = ws[0][0].shape[1]
    per_step = 2
    tile = pl.BlockSpec((per_step, slots, BLK, BLK), lambda i: (i, 0, 0, 0))
    h_spec = pl.BlockSpec((1, per_step, count, BLK), lambda i: (which, i, 0, 0))
    return pl.pallas_call(
        functools.partial(spread_kernel, n, firsts, which, per_step),
        grid=(per_chunk // per_step,),
        in_specs=[smem()] * 2 + [h_spec] * chunks + [tile] * (chunks * n),
        out_specs=whole((count, width)),
        out_shape=jax.ShapeDtypeStruct((count, width), jnp.bfloat16),
        scratch_shapes=[pltpu.VMEM((count, width), jnp.float32)],
        compiler_params=params(),
        cost_estimate=pl.CostEstimate(flops=0, bytes_accessed=MIB // 64, transcendentals=0),
        name="spread",
    )(me, index, *hs, *[w for chunk in ws for w in chunk])


def finish(first, blocks, up, down, got, done):
    per_chunk, slots = up.shape[:2]
    per_step = 4
    at = first // per_step
    own = pl.BlockSpec((per_step, slots, BLK, BLK), lambda i: (i, 0, 0, 0))
    sent = pl.BlockSpec((2, per_step, slots, BLK, BLK), lambda i: (0, i, 0, 0, 0))
    part = pl.BlockSpec((per_step, slots, BLK, BLK), lambda i: (at + i, 0, 0, 0))
    kept = pl.BlockSpec(memory_space=pl.ANY)
    shape = jax.ShapeDtypeStruct((blocks, slots, BLK, BLK), jnp.float32)
    return pl.pallas_call(
        functools.partial(finish_kernel, len(got)),
        grid=(per_chunk // per_step,),
        in_specs=[own] * 2 + [sent] * len(got) + [kept] * len(done),
        out_specs=[part] * 2,
        out_shape=[shape] * 2,
        input_output_aliases={2 + len(got) + i: i for i in range(len(done))},
        compiler_params=params(),
        cost_estimate=pl.CostEstimate(flops=0, bytes_accessed=MIB // 64, transcendentals=0),
        name="finish_chunk",
    )(up, down, *got, *done)


def after(a, *earlier):
    return lax.optimization_barrier((a,) + earlier)[0]


def exchange(a, bit, n):
    return lax.ppermute(a, "fsdp", [(i, i ^ bit) for i in range(n)])


def gather(n, a, bits):
    held = {0: a}
    for bit in bits:
        for r in list(held):
            if r ^ bit not in held:
                held[r ^ bit] = exchange(held[r], bit, n)
    return [held[r] for r in range(n)]


def body(n, tokens, out_grad, up_weight, down_weight, up_index, down_index):
    width = tokens.shape[1]
    blocks = up_weight.shape[0]
    chunks = CHUNKS
    per_chunk = blocks // chunks
    firsts = [c * per_chunk for c in range(chunks)]
    bits = [1 << b for b in range(n.bit_length() - 1)]
    me = lax.axis_index("fsdp").astype(jnp.int32).reshape(1)

    both = jnp.concatenate([tokens, out_grad], axis=1)
    mine = lax.all_gather(both, "tensor", axis=0, tiled=True)
    swapped = exchange(both, 1, n)

    ups, downs, hs = [], [], []
    for c in range(chunks):
        part = slice(firsts[c], firsts[c] + per_chunk)
        ups.append(gather(n, up_weight[part], bits))
        downs.append(gather(n, down_weight[part], bits[::-1]))
        if c == 0:
            marks = [ups[0][bits[0]], ups[0][bits[-1]], downs[0][bits[0]], downs[0][bits[-1]]]
            other = lax.all_gather(after(swapped, *marks), "tensor", axis=0, tiled=True)
        hs.append(forward(n, firsts[c], me, up_index, down_index, mine, ups[c], downs[c]))

    mixed = spread(n, 0, firsts, me, down_index, hs, downs, width)
    mixed_rows = lax.psum_scatter(mixed, "tensor", scatter_dimension=0, tiled=True)

    grad_out = ()
    for c in range(chunks):
        rows = other
        if c == 0:
            rows = after(other, mixed)
        if c == 1:
            rows = after(other, spread_in)
        up, down, *sent = grads(
            n, firsts[c], me, up_index, down_index, mine, rows, hs[c], ups[c], downs[c]
        )
        if c == 0:
            h_last = after(hs[-1], sent[0])
            spread_in = spread(n, 1, firsts, me, up_index, hs[:-1] + [h_last], ups, width)
            input_rows = lax.psum_scatter(spread_in, "tensor", scatter_dimension=0, tiled=True)
        got = [exchange(part, 2 * (e + 1), n) for e, part in enumerate(sent)]
        grad_out = finish(firsts[c], blocks, up, down, got, grad_out)
    return (mixed_rows, input_rows, *grad_out)


def solution(mesh):
    return jax.shard_map(
        functools.partial(body, mesh.shape["fsdp"]),
        mesh=mesh,
        in_specs=(
            P(("fsdp", "tensor"), None),
            P(("fsdp", "tensor"), None),
            P("tensor", "fsdp", None, None),
            P("tensor", "fsdp", None, None),
            P("tensor", None),
            P("tensor", None),
        ),
        out_specs=(
            P(("fsdp", "tensor"), None),
            P(("fsdp", "tensor"), None),
            P("tensor", "fsdp", None, None),
            P("tensor", "fsdp", None, None),
        ),
        check_vma=False,
    )
```

time: 349 us -> 318 us (0.911)
  Pallas kernels: 79.3 us -> 113 us
  local copies, waits for them, and re-layouts: 43.1 us -> 9.93 us
  starting transfers between devices: 47.2 us -> 37.1 us
  other arithmetic: 9.69 us -> 0 us
  waiting for transfers between devices: 153 us -> 144 us
    unnamed x141 -> x65, local copies, waits for them, and re-layouts: 40 us -> 7.06 us
    pallas_call x4, Pallas kernels: 31.8 us -> 47.8 us  [grads(): pl.pallas_call(functools.partial(grad_kernel, n, first, per_step), grid=(...]
    pallas_call x2 -> x6, Pallas kernels: 23.7 us -> 35.5 us  [the longest x2 23.9 us: spread(): pl.pallas_call(functools.partial(spread_kernel, n, firsts, which, per_ste...]
    ppermute x33 -> x29, starting transfers between devices: 46.8 us -> 36.7 us  [exchange(): return lax.ppermute(a, 'fsdp', [(i, i ^ bit) for i in range(n)])]
    ppermute x33 -> x29, waiting for transfers between devices: 153 us -> 144 us  [exchange(): return lax.ppermute(a, 'fsdp', [(i, i ^ bit) for i in range(n)])]
    pallas_call x4, Pallas kernels: 23.7 us -> 29.6 us  [forward(): pl.pallas_call(functools.partial(forward_kernel, n, first, per_step), gri...]
    convert_element_type x4 -> x0, other arithmetic: 4.57 us -> none  [body(): got = exchange(part, 2 * (e + 1), n).astype(jnp.float32)]
    concatenate x1 -> x0, other arithmetic: 3.85 us -> none  [body(): up_grad = jnp.concatenate(ups_grad, axis=0)]
  transfers between devices with their start and end apart: 37 -> 33, of which waited for: 17 -> 15; matrix products, arithmetic and copies ran while one was open for 3% -> 1% of each run, Pallas kernels for 23% -> 36%
where the time goes in v1:
time: 318 us
  waiting for transfers between devices  144 us (45%)
  Pallas kernels  113 us (36%)
  starting transfers between devices  37.1 us (12%)
  between operations  14.1 us (4%)
  local copies, waits for them, and re-layouts  9.93 us (3%)
    ppermute x29, waiting for transfers between devices, exchange(): return lax.ppermute(a, 'fsdp', [(i, i ^ bit) for i in range(n)])  144 us
    pallas_call x4, Pallas kernels, grads(): pl.pallas_call(functools.partial(grad_kernel, n, first, per_step), grid=(...  47.8 us
    ppermute x29, starting transfers between devices, exchange(): return lax.ppermute(a, 'fsdp', [(i, i ^ bit) for i in range(n)])  36.7 us
    pallas_call x4, Pallas kernels, forward(): pl.pallas_call(functools.partial(forward_kernel, n, first, per_step), gri...  29.6 us
    pallas_call x2, Pallas kernels, spread(): pl.pallas_call(functools.partial(spread_kernel, n, firsts, which, per_ste...  23.9 us
    pallas_call x4, Pallas kernels, finish(): pl.pallas_call(functools.partial(finish_kernel, len(got)), grid=(per_chun...  11.6 us
    unnamed x65, local copies, waits for them, and re-layouts  7.06 us
  transfers between devices with their start and end apart: 33, of which 15 were waited for; matrix products, arithmetic and copies ran while one was open for 1% of the time, Pallas kernels for 36%

profile of v1, /device:TPU:0, one launch (start us, length us, event | category | flops | bytes accessed | tf_op | source)
XLA Modules:
  0.0 317.7 jit_solution(13512480176967153150)
XLA Ops:
  10.3 3.0 collective-permute-start.24
  19.6 10.3 %collective-permute-done.1.refs_2_.refs_6_ = bf16[8,2,128,128]{3,2,1,0:T(8,128)(2,1)S(1)} collective-permute-done((bf16[8,2,128,128]{3,2,1,0:T(8,128)(2,1)S(1)}, bf16[8,2,128,128]{3,2,1,0:T(8,128)(2,1)S(1)}, u32[]{:S(2)}, u32[]{:S(2)}) %collective-permute-start.1) | collective-permute-done | bytes 524320 | tf_op jit(solution)/shard_map/ppermute | solution.py:227
  29.9 13.2 %collective-permute-done.refs_1_.refs_5_ = bf16[8,2,128,128]{3,2,1,0:T(8,128)(2,1)S(1)} collective-permute-done((bf16[8,2,128,128]{3,2,1,0:T(8,128)(2,1)S(1)}, bf16[8,2,128,128]{3,2,1,0:T(8,128)(2,1)S(1)}, u32[]{:S(2)}, u32[]{:S(2)}) %collective-permute-start) | collective-permute-done | bytes 524320 | tf_op jit(solution)/shard_map/ppermute | solution.py:227
  43.1 10.4 %collective-permute-done.3.refs_5_ = bf16[8,2,128,128]{3,2,1,0:T(8,128)(2,1)S(1)} collective-permute-done((bf16[8,2,128,128]{3,2,1,0:T(8,128)(2,1)S(1)}, bf16[8,2,128,128]{3,2,1,0:T(8,128)(2,1)S(1)}, u32[]{:S(2)}, u32[]{:S(2)}) %collective-permute-start.3) | collective-permute-done | bytes 524320 | tf_op jit(solution)/shard_map/ppermute | solution.py:227
  54.4 1.8 collective-permute-start.18
  60.2 9.2 %collective-permute-done.18.refs_1_.refs_17_ = bf16[8,2,128,128]{3,2,1,0:T(8,128)(2,1)} collective-permute-done((bf16[8,2,128,128]{3,2,1,0:T(8,128)(2,1)S(1)}, bf16[8,2,128,128]{3,2,1,0:T(8,128)(2,1)}, u32[]{:S(2)}, u32[]{:S(2)}) %collective-permute-start.18) | collective-permute-done | bytes 524320 | tf_op jit(solution)/shard_map/ppermute | solution.py:227
  69.4 1.8 collective-permute-start.22
  72.6 8.0 %collective-permute-done.6.refs_1_.refs_9_ = bf16[8,2,128,128]{3,2,1,0:T(8,128)(2,1)S(1)} collective-permute-done((bf16[8,2,128,128]{3,2,1,0:T(8,128)(2,1)S(1)}, bf16[8,2,128,128]{3,2,1,0:T(8,128)(2,1)S(1)}, u32[]{:S(2)}, u32[]{:S(2)}) %collective-permute-start.6) | collective-permute-done | bytes 524320 | tf_op jit(solution)/shard_map/ppermute | solution.py:227
  83.8 8.0 %collective-permute-done.12.refs_1_.refs_13_ = bf16[8,2,128,128]{3,2,1,0:T(8,128)(2,1)S(1)} collective-permute-done((bf16[8,2,128,128]{3,2,1,0:T(8,128)(2,1)S(1)}, bf16[8,2,128,128]{3,2,1,0:T(8,128)(2,1)S(1)}, u32[]{:S(2)}, u32[]{:S(2)}) %collective-permute-start.12) | collective-permute-done | bytes 524320 | tf_op jit(solution)/shard_map/ppermute | solution.py:227
  95.1 9.7 %collective-permute-done.10.refs_6_.refs_10_ = bf16[8,2,128,128]{3,2,1,0:T(8,128)(2,1)} collective-permute-done((bf16[8,2,128,128]{3,2,1,0:T(8,128)(2,1)S(1)}, bf16[8,2,128,128]{3,2,1,0:T(8,128)(2,1)}, u32[]{:S(2)}, u32[]{:S(2)}) %collective-permute-start.10) | collective-permute-done | bytes 524320 | tf_op jit(solution)/shard_map/ppermute | solution.py:227
  106.9 9.1 %collective-permute-done.16.refs_6_.refs_14_ = bf16[8,2,128,128]{3,2,1,0:T(8,128)(2,1)S(1)} collective-permute-done((bf16[8,2,128,128]{3,2,1,0:T(8,128)(2,1)S(1)}, bf16[8,2,128,128]{3,2,1,0:T(8,128)(2,1)S(1)}, u32[]{:S(2)}, u32[]{:S(2)}) %collective-permute-start.16) | collective-permute-done | bytes 524320 | tf_op jit(solution)/shard_map/ppermute | solution.py:227
  118.0 9.2 %collective-permute-done.8.refs_3_.refs_11_ = bf16[8,2,128,128]{3,2,1,0:T(8,128)(2,1)S(1)} collective-permute-done((bf16[8,2,128,128]{3,2,1,0:T(8,128)(2,1)S(1)}, bf16[8,2,128,128]{3,2,1,0:T(8,128)(2,1)S(1)}, u32[]{:S(2)}, u32[]{:S(2)}) %collective-permute-start.8) | collective-permute-done | bytes 524320 | tf_op jit(solution)/shard_map/ppermute | solution.py:227
  128.7 9.7 %collective-permute-done.2.refs_3_.refs_7_ = bf16[8,2,128,128]{3,2,1,0:T(8,128)(2,1)S(1)} collective-permute-done((bf16[8,2,128,128]{3,2,1,0:T(8,128)(2,1)}, bf16[8,2,128,128]{3,2,1,0:T(8,128)(2,1)S(1)}, u32[]{:S(2)}, u32[]{:S(2)}) %collective-permute-start.2) | collective-permute-done | bytes 524320 | tf_op jit(solution)/shard_map/ppermute | solution.py:227
  138.7 10.9 %collective-permute-done.14.refs_3_.refs_15_ = bf16[8,2,128,128]{3,2,1,0:T(8,128)(2,1)S(1)} collective-permute-done((bf16[8,2,128,128]{3,2,1,0:T(8,128)(2,1)S(1)}, bf16[8,2,128,128]{3,2,1,0:T(8,128)(2,1)S(1)}, u32[]{:S(2)}, u32[]{:S(2)}) %collective-permute-start.14) | collective-permute-done | bytes 524320 | tf_op jit(solution)/shard_map/ppermute | solution.py:227
  150.0 1.8 collective-permute-start.20
  154.8 7.4 %forward_chunk.4.refs_0_.h_mine = bf16[2,8,192,128]{3,2,1,0:T(8,128)(2,1)} custom-call(s32[1]{0:T(128)} %bitcast.me_ref, s32[32,8]{1,0:T(8,128)} %copy.16.up_idx.idx, s32[32,8]{1,0:T(8,128)} %copy.24.down_idx.idx, bf16[192,16384]{1,0:T(8,128)(2,1)} %all-gather.3.cloned.1.call-done.rows.mine, bf16[8,2,128,128]{3,2,1,0:T(8,128)(2,1)} %copy-done.6, ...), custom_call_target="tpu_custom_call" | custom-call | bytes 16384 | tf_op jit(solution)/shard_map/forward_chunk/pallas_call | solution.py:147
  162.3 7.4 %forward_chunk.6.refs_2_.h_mine = bf16[2,8,192,128]{3,2,1,0:T(8,128)(2,1)} custom-call(s32[1]{0:T(128)} %bitcast.me_ref, s32[32,8]{1,0:T(8,128)} %copy.16.up_idx.idx, s32[32,8]{1,0:T(8,128)} %copy.24.down_idx.idx, bf16[192,16384]{1,0:T(8,128)(2,1)} %all-gather.3.cloned.1.call-done.rows.mine, bf16[8,2,128,128]{3,2,1,0:T(8,128)(2,1)} %copy-done.2, ...), custom_call_target="tpu_custom_call" | custom-call | bytes 16384 | tf_op jit(solution)/shard_map/forward_chunk/pallas_call | solution.py:147
  169.7 7.4 %forward_chunk.5.refs_1_.h_mine = bf16[2,8,192,128]{3,2,1,0:T(8,128)(2,1)} custom-call(s32[1]{0:T(128)} %bitcast.me_ref, s32[32,8]{1,0:T(8,128)} %copy.16.up_idx.idx, s32[32,8]{1,0:T(8,128)} %copy.24.down_idx.idx, bf16[192,16384]{1,0:T(8,128)(2,1)} %all-gather.3.cloned.1.call-done.rows.mine, bf16[8,2,128,128]{3,2,1,0:T(8,128)(2,1)} %copy-done.4, ...), custom_call_target="tpu_custom_call" | custom-call | bytes 16384 | tf_op jit(solution)/shard_map/forward_chunk/pallas_call | solution.py:147
  177.1 7.4 %forward_chunk.7.refs_3_.h_mine = bf16[2,8,192,128]{3,2,1,0:T(8,128)(2,1)} custom-call(s32[1]{0:T(128)} %bitcast.me_ref, s32[32,8]{1,0:T(8,128)} %copy.16.up_idx.idx, s32[32,8]{1,0:T(8,128)} %copy.24.down_idx.idx, bf16[192,16384]{1,0:T(8,128)(2,1)} %all-gather.3.cloned.1.call-done.rows.mine, bf16[8,2,128,128]{3,2,1,0:T(8,128)(2,1)} %copy-done, ...), custom_call_target="tpu_custom_call" | custom-call | bytes 16384 | tf_op jit(solution)/shard_map/forward_chunk/pallas_call | solution.py:147
  184.5 12.0 %spread.2 = bf16[192,8192]{1,0:T(8,128)(2,1)} custom-call(s32[1]{0:T(128)} %bitcast.me_ref, s32[32,8]{1,0:T(8,128)} %copy.24.down_idx.idx, bf16[2,8,192,128]{3,2,1,0:T(8,128)(2,1)} %forward_chunk.4.refs_0_.h_mine, bf16[2,8,192,128]{3,2,1,0:T(8,128)(2,1)} %forward_chunk.5.refs_1_.h_mine, bf16[2,8,192,128]{3,2,1,0:T(8,128)(2,1)} %forward_chunk.6.refs_2_.h_mine, ...), custom_call_target="tpu_custom_call" | custom-call | bytes 16384 | tf_op jit(solution)/shard_map/spread/pallas_call | solution.py:187
  196.8 11.8 %grad_chunk.4 = (f32[8,2,128,128]{3,2,1,0:T(8,128)}, f32[8,2,128,128]{3,2,1,0:T(8,128)}, bf16[2,8,2,128,128]{4,3,2,1,0:T(8,128)(2,1)}) custom-call(s32[1]{0:T(128)} %bitcast.me_ref, s32[32,8]{1,0:T(8,128)} %copy.16.up_idx.idx, s32[32,8]{1,0:T(8,128)} %copy.24.down_idx.idx, bf16[192,16384]{1,0:T(8,128)(2,1)} %all-gather.3.cloned.1.call-done.rows.mine, ...), custom_call_target="tpu_custom_call" | custom-call | bytes 16384 | tf_op jit(solution)/shard_map/grad_chunk/pallas_call | solution.py:168
  208.6 11.9 %spread.3 = bf16[192,8192]{1,0:T(8,128)(2,1)} custom-call(s32[1]{0:T(128)} %bitcast.me_ref, s32[32,8]{1,0:T(8,128)} %copy.16.up_idx.idx, bf16[2,8,192,128]{3,2,1,0:T(8,128)(2,1)} %forward_chunk.4.refs_0_.h_mine, bf16[2,8,192,128]{3,2,1,0:T(8,128)(2,1)} %forward_chunk.5.refs_1_.h_mine, bf16[2,8,192,128]{3,2,1,0:T(8,128)(2,1)} %forward_chunk.6.refs_2_.h_mine, ...), custom_call_target="tpu_custom_call" | custom-call | bytes 16384 | tf_op jit(solution)/shard_map/spread/pallas_call | solution.py:187
  221.2 12.0 %grad_chunk.7 = (f32[8,2,128,128]{3,2,1,0:T(8,128)}, f32[8,2,128,128]{3,2,1,0:T(8,128)}, bf16[2,8,2,128,128]{4,3,2,1,0:T(8,128)(2,1)}) custom-call(s32[1]{0:T(128)} %bitcast.me_ref, s32[32,8]{1,0:T(8,128)} %copy.16.up_idx.idx, s32[32,8]{1,0:T(8,128)} %copy.24.down_idx.idx, bf16[192,16384]{1,0:T(8,128)(2,1)} %all-gather.3.cloned.1.call-done.rows.mine, ...), custom_call_target="tpu_custom_call" | custom-call | bytes 16384 | tf_op jit(solution)/shard_map/grad_chunk/pallas_call | solution.py:168
  234.7 12.0 %grad_chunk.6 = (f32[8,2,128,128]{3,2,1,0:T(8,128)}, f32[8,2,128,128]{3,2,1,0:T(8,128)}, bf16[2,8,2,128,128]{4,3,2,1,0:T(8,128)(2,1)}) custom-call(s32[1]{0:T(128)} %bitcast.me_ref, s32[32,8]{1,0:T(8,128)} %copy.16.up_idx.idx, s32[32,8]{1,0:T(8,128)} %copy.24.down_idx.idx, bf16[192,16384]{1,0:T(8,128)(2,1)} %all-gather.3.cloned.1.call-done.rows.mine, ...), custom_call_target="tpu_custom_call" | custom-call | bytes 16384 | tf_op jit(solution)/shard_map/grad_chunk/pallas_call | solution.py:168
  247.3 12.0 %grad_chunk.5 = (f32[8,2,128,128]{3,2,1,0:T(8,128)}, f32[8,2,128,128]{3,2,1,0:T(8,128)}, bf16[2,8,2,128,128]{4,3,2,1,0:T(8,128)(2,1)}) custom-call(s32[1]{0:T(128)} %bitcast.me_ref, s32[32,8]{1,0:T(8,128)} %copy.16.up_idx.idx, s32[32,8]{1,0:T(8,128)} %copy.24.down_idx.idx, bf16[192,16384]{1,0:T(8,128)(2,1)} %all-gather.3.cloned.1.call-done.rows.mine, ...), custom_call_target="tpu_custom_call" | custom-call | bytes 16384 | tf_op jit(solution)/shard_map/grad_chunk/pallas_call | solution.py:168
  261.8 2.9 finish_chunk.4
  264.7 4.7 %collective-permute-done.27.refs_0_ = bf16[2,8,2,128,128]{4,3,2,1,0:T(8,128)(2,1)S(1)} collective-permute-done((bf16[2,8,2,128,128]{4,3,2,1,0:T(8,128)(2,1)}, bf16[2,8,2,128,128]{4,3,2,1,0:T(8,128)(2,1)S(1)}, u32[]{:S(2)}, u32[]{:S(2)}) %collective-permute-start.27) | collective-permute-done | bytes 1048608 | tf_op jit(solution)/shard_map/ppermute | solution.py:227
  270.4 2.9 finish_chunk.5
  273.3 18.6 %collective-permute-done.26.refs_0_ = bf16[2,8,2,128,128]{4,3,2,1,0:T(8,128)(2,1)S(1)} collective-permute-done((bf16[2,8,2,128,128]{4,3,2,1,0:T(8,128)(2,1)}, bf16[2,8,2,128,128]{4,3,2,1,0:T(8,128)(2,1)S(1)}, u32[]{:S(2)}, u32[]{:S(2)}) %collective-permute-start.26) | collective-permute-done | bytes 1048608 | tf_op jit(solution)/shard_map/ppermute | solution.py:227
  292.8 2.9 finish_chunk.6
  295.7 12.6 %collective-permute-done.25.refs_0_ = bf16[2,8,2,128,128]{4,3,2,1,0:T(8,128)(2,1)} collective-permute-done((bf16[2,8,2,128,128]{4,3,2,1,0:T(8,128)(2,1)}, bf16[2,8,2,128,128]{4,3,2,1,0:T(8,128)(2,1)}, u32[]{:S(2)}, u32[]{:S(2)}) %collective-permute-start.25) | collective-permute-done | bytes 1048608 | tf_op jit(solution)/shard_map/ppermute | solution.py:227
  308.3 2.9 finish_chunk.7
  (120 shorter events, 38.8 us)
Async XLA Ops:
  7.2 147.6 %all-gather.3.cloned.1.call-start = ((), (), s32[]{:S(2)}) async-start(), calls=%async_computation.2 | async-start | bytes 7077888 | tf_op jit(solution)/shard_map/all_gather | solution.py:249
  10.2 186.6 %all-gather.5.cloned.1.call-start = ((), (), s32[]{:S(2)}) async-start(), calls=%async_computation.4 | async-start | bytes 7077888 | tf_op jit(solution)/shard_map/all_gather | solution.py:259
  10.3 44.0 %collective-permute-start.24 = (bf16[24,16384]{1,0:T(8,128)(2,1)}, bf16[24,16384]{1,0:T(8,128)(2,1)}, u32[]{:S(2)}, u32[]{:S(2)}) collective-permute-start(bf16[24,16384]{1,0:T(8,128)(2,1)} %copy-done.25), channel_id=1, source_target_pairs={{0,8},{8,0},{16,24},{24,16},{1,9},{9,1},{17,25},{25,17},{2,10},{10... | collective-permute-start | bytes 2359304 | tf_op jit(solution)/shard_map/ppermute | solution.py:227
  16.6 26.5 %collective-permute-start = (bf16[8,2,128,128]{3,2,1,0:T(8,128)(2,1)S(1)}, bf16[8,2,128,128]{3,2,1,0:T(8,128)(2,1)S(1)}, u32[]{:S(2)}, u32[]{:S(2)}) collective-permute-start(bf16[8,2,128,128]{3,2,1,0:T(8,128)(2,1)S(1)} %get-tuple-element.58.refs_0_.refs_4_), channel_id=1, source_target_pairs={{0,8},{8,0},{16,24},{24,16},{1,9},{9,1},{17,25},{25,17},{2,10},{10... | collective-permute-start | bytes 1572872 | tf_op jit(solution)/shard_map/ppermute | solution.py:227
  17.4 25.7 %collective-permute-start.4 = (bf16[8,2,128,128]{3,2,1,0:T(8,128)(2,1)S(1)}, bf16[8,2,128,128]{3,2,1,0:T(8,128)(2,1)S(1)}, u32[]{:S(2)}, u32[]{:S(2)}) collective-permute-start(bf16[8,2,128,128]{3,2,1,0:T(8,128)(2,1)S(1)} %get-tuple-element.54.refs_4_), channel_id=1, source_target_pairs={{0,16},{8,24},{16,0},{24,8},{1,17},{9,25},{17,1},{25,9},{2,18},{10... | collective-permute-start | bytes 1572872 | tf_op jit(solution)/shard_map/ppermute | solution.py:227
  18.1 35.4 %collective-permute-start.3 = (bf16[8,2,128,128]{3,2,1,0:T(8,128)(2,1)S(1)}, bf16[8,2,128,128]{3,2,1,0:T(8,128)(2,1)S(1)}, u32[]{:S(2)}, u32[]{:S(2)}) collective-permute-start(bf16[8,2,128,128]{3,2,1,0:T(8,128)(2,1)S(1)} %get-tuple-element.54.refs_4_), channel_id=1, source_target_pairs={{0,8},{8,0},{16,24},{24,16},{1,9},{9,1},{17,25},{25,17},{2,10},{10... | collective-permute-start | bytes 1572872 | tf_op jit(solution)/shard_map/ppermute | solution.py:227
  54.3 256.9 %reduce-scatter.3.cloned.1.call-start = ((), (), s32[]{:S(2)}) async-start(), calls=%async_computation.3 | async-start | bytes 3538944 | tf_op jit(solution)/shard_map/reduce_scatter | solution.py:263
  54.4 15.0 %collective-permute-start.18 = (bf16[8,2,128,128]{3,2,1,0:T(8,128)(2,1)S(1)}, bf16[8,2,128,128]{3,2,1,0:T(8,128)(2,1)}, u32[]{:S(2)}, u32[]{:S(2)}) collective-permute-start(bf16[8,2,128,128]{3,2,1,0:T(8,128)(2,1)S(1)} %get-tuple-element.56.refs_0_.refs_16_), channel_id=1, source_target_pairs={{0,8},{8,0},{16,24},{24,16},{1,9},{9,1},{17,25},{25,17},{2,10},{10... | collective-permute-start | bytes 1572872 | tf_op jit(solution)/shard_map/ppermute | solution.py:227
  56.2 15.0 %collective-permute-start.7 = (bf16[8,2,128,128]{3,2,1,0:T(8,128)(2,1)S(1)}, bf16[8,2,128,128]{3,2,1,0:T(8,128)(2,1)S(1)}, u32[]{:S(2)}, u32[]{:S(2)}) collective-permute-start(bf16[8,2,128,128]{3,2,1,0:T(8,128)(2,1)S(1)} %get-tuple-element.57.refs_0_.refs_8_), channel_id=1, source_target_pairs={{0,16},{8,24},{16,0},{24,8},{1,17},{9,25},{17,1},{25,9},{2,18},{10... | collective-permute-start | bytes 1572872 | tf_op jit(solution)/shard_map/ppermute | solution.py:227
  57.7 22.8 %collective-permute-start.6 = (bf16[8,2,128,128]{3,2,1,0:T(8,128)(2,1)S(1)}, bf16[8,2,128,128]{3,2,1,0:T(8,128)(2,1)S(1)}, u32[]{:S(2)}, u32[]{:S(2)}) collective-permute-start(bf16[8,2,128,128]{3,2,1,0:T(8,128)(2,1)S(1)} %get-tuple-element.57.refs_0_.refs_8_), channel_id=1, source_target_pairs={{0,8},{8,0},{16,24},{24,16},{1,9},{9,1},{17,25},{25,17},{2,10},{10... | collective-permute-start | bytes 1572872 | tf_op jit(solution)/shard_map/ppermute | solution.py:227
  58.2 24.0 %collective-permute-start.13 = (bf16[8,2,128,128]{3,2,1,0:T(8,128)(2,1)S(1)}, bf16[8,2,128,128]{3,2,1,0:T(8,128)(2,1)S(1)}, u32[]{:S(2)}, u32[]{:S(2)}) collective-permute-start(bf16[8,2,128,128]{3,2,1,0:T(8,128)(2,1)S(1)} %get-tuple-element.59.refs_0_.refs_12_), channel_id=1, source_target_pairs={{0,16},{8,24},{16,0},{24,8},{1,17},{9,25},{17,1},{25,9},{2,18},{10... | collective-permute-start | bytes 1572872 | tf_op jit(solution)/shard_map/ppermute | solution.py:227
  58.5 33.3 %collective-permute-start.12 = (bf16[8,2,128,128]{3,2,1,0:T(8,128)(2,1)S(1)}, bf16[8,2,128,128]{3,2,1,0:T(8,128)(2,1)S(1)}, u32[]{:S(2)}, u32[]{:S(2)}) collective-permute-start(bf16[8,2,128,128]{3,2,1,0:T(8,128)(2,1)S(1)} %get-tuple-element.59.refs_0_.refs_12_), channel_id=1, source_target_pairs={{0,8},{8,0},{16,24},{24,16},{1,9},{9,1},{17,25},{25,17},{2,10},{10... | collective-permute-start | bytes 1572872 | tf_op jit(solution)/shard_map/ppermute | solution.py:227
  69.4 24.2 %collective-permute-start.22 = (bf16[8,2,128,128]{3,2,1,0:T(8,128)(2,1)S(1)}, bf16[8,2,128,128]{3,2,1,0:T(8,128)(2,1)}, u32[]{:S(2)}, u32[]{:S(2)}) collective-permute-start(bf16[8,2,128,128]{3,2,1,0:T(8,128)(2,1)S(1)} %get-tuple-element.52.refs_4_.refs_16_), channel_id=1, source_target_pairs={{0,16},{8,24},{16,0},{24,8},{1,17},{9,25},{17,1},{25,9},{2,18},{10... | collective-permute-start | bytes 1572872 | tf_op jit(solution)/shard_map/ppermute | solution.py:227
  71.2 33.7 %collective-permute-start.10 = (bf16[8,2,128,128]{3,2,1,0:T(8,128)(2,1)S(1)}, bf16[8,2,128,128]{3,2,1,0:T(8,128)(2,1)}, u32[]{:S(2)}, u32[]{:S(2)}) collective-permute-start(bf16[8,2,128,128]{3,2,1,0:T(8,128)(2,1)S(1)} %get-tuple-element.53.refs_4_.refs_8_), channel_id=1, source_target_pairs={{0,16},{8,24},{16,0},{24,8},{1,17},{9,25},{17,1},{25,9},{2,18},{10... | collective-permute-start | bytes 1572872 | tf_op jit(solution)/shard_map/ppermute | solution.py:227
  80.5 25.8 %collective-permute-start.9 = (bf16[8,2,128,128]{3,2,1,0:T(8,128)(2,1)S(1)}, bf16[8,2,128,128]{3,2,1,0:T(8,128)(2,1)S(1)}, u32[]{:S(2)}, u32[]{:S(2)}) collective-permute-start(bf16[8,2,128,128]{3,2,1,0:T(8,128)(2,1)S(1)} %get-tuple-element.53.refs_4_.refs_8_), channel_id=1, source_target_pairs={{0,8},{8,0},{16,24},{24,16},{1,9},{9,1},{17,25},{25,17},{2,10},{10... | collective-permute-start | bytes 1572872 | tf_op jit(solution)/shard_map/ppermute | solution.py:227
  82.3 33.7 %collective-permute-start.16 = (bf16[8,2,128,128]{3,2,1,0:T(8,128)(2,1)S(1)}, bf16[8,2,128,128]{3,2,1,0:T(8,128)(2,1)S(1)}, u32[]{:S(2)}, u32[]{:S(2)}) collective-permute-start(bf16[8,2,128,128]{3,2,1,0:T(8,128)(2,1)S(1)} %get-tuple-element.55.refs_4_.refs_12_), channel_id=1, source_target_pairs={{0,16},{8,24},{16,0},{24,8},{1,17},{9,25},{17,1},{25,9},{2,18},{10... | collective-permute-start | bytes 1572872 | tf_op jit(solution)/shard_map/ppermute | solution.py:227
  91.8 24.5 %collective-permute-start.15 = (bf16[8,2,128,128]{3,2,1,0:T(8,128)(2,1)S(1)}, bf16[8,2,128,128]{3,2,1,0:T(8,128)(2,1)S(1)}, u32[]{:S(2)}, u32[]{:S(2)}) collective-permute-start(bf16[8,2,128,128]{3,2,1,0:T(8,128)(2,1)S(1)} %get-tuple-element.55.refs_4_.refs_12_), channel_id=1, source_target_pairs={{0,8},{8,0},{16,24},{24,16},{1,9},{9,1},{17,25},{25,17},{2,10},{10... | collective-permute-start | bytes 1572872 | tf_op jit(solution)/shard_map/ppermute | solution.py:227
  93.6 33.6 %collective-permute-start.8 = (bf16[8,2,128,128]{3,2,1,0:T(8,128)(2,1)S(1)}, bf16[8,2,128,128]{3,2,1,0:T(8,128)(2,1)S(1)}, u32[]{:S(2)}, u32[]{:S(2)}) collective-permute-start(bf16[8,2,128,128]{3,2,1,0:T(8,128)(2,1)S(1)} %collective-permute-done.6.refs_1_.refs_9_), channel_id=1, source_target_pairs={{0,16},{8,24},{16,0},{24,8},{1,17},{9,25},{17,1},{25,9},{2,18},{10... | collective-permute-start | bytes 1572872 | tf_op jit(solution)/shard_map/ppermute | solution.py:227
  104.9 33.6 %collective-permute-start.2 = (bf16[8,2,128,128]{3,2,1,0:T(8,128)(2,1)}, bf16[8,2,128,128]{3,2,1,0:T(8,128)(2,1)S(1)}, u32[]{:S(2)}, u32[]{:S(2)}) collective-permute-start(bf16[8,2,128,128]{3,2,1,0:T(8,128)(2,1)} %copy-done.9), channel_id=1, source_target_pairs={{0,16},{8,24},{16,0},{24,8},{1,17},{9,25},{17,1},{25,9},{2,18},{10... | collective-permute-start | bytes 1572872 | tf_op jit(solution)/shard_map/ppermute | solution.py:227
  106.4 43.3 %collective-permute-start.14 = (bf16[8,2,128,128]{3,2,1,0:T(8,128)(2,1)S(1)}, bf16[8,2,128,128]{3,2,1,0:T(8,128)(2,1)S(1)}, u32[]{:S(2)}, u32[]{:S(2)}) collective-permute-start(bf16[8,2,128,128]{3,2,1,0:T(8,128)(2,1)S(1)} %collective-permute-done.12.refs_1_.refs_13_), channel_id=1, source_target_pairs={{0,16},{8,24},{16,0},{24,8},{1,17},{9,25},{17,1},{25,9},{2,18},{10... | collective-permute-start | bytes 1572872 | tf_op jit(solution)/shard_map/ppermute | solution.py:227
  116.0 34.0 %collective-permute-start.5 = (bf16[8,2,128,128]{3,2,1,0:T(8,128)(2,1)}, bf16[8,2,128,128]{3,2,1,0:T(8,128)(2,1)S(1)}, u32[]{:S(2)}, u32[]{:S(2)}) collective-permute-start(bf16[8,2,128,128]{3,2,1,0:T(8,128)(2,1)} %copy-done.10), channel_id=1, source_target_pairs={{0,8},{8,0},{16,24},{24,16},{1,9},{9,1},{17,25},{25,17},{2,10},{10... | collective-permute-start | bytes 1572872 | tf_op jit(solution)/shard_map/ppermute | solution.py:227
  116.3 35.6 %collective-permute-start.17 = (bf16[8,2,128,128]{3,2,1,0:T(8,128)(2,1)S(1)}, bf16[8,2,128,128]{3,2,1,0:T(8,128)(2,1)S(1)}, u32[]{:S(2)}, u32[]{:S(2)}) collective-permute-start(bf16[8,2,128,128]{3,2,1,0:T(8,128)(2,1)S(1)} %collective-permute-done.16.refs_6_.refs_14_), channel_id=1, source_target_pairs={{0,8},{8,0},{16,24},{24,16},{1,9},{9,1},{17,25},{25,17},{2,10},{10... | collective-permute-start | bytes 1572872 | tf_op jit(solution)/shard_map/ppermute | solution.py:227
  127.2 49.9 %collective-permute-start.19 = (bf16[8,2,128,128]{3,2,1,0:T(8,128)(2,1)S(1)}, bf16[8,2,128,128]{3,2,1,0:T(8,128)(2,1)}, u32[]{:S(2)}, u32[]{:S(2)}) collective-permute-start(bf16[8,2,128,128]{3,2,1,0:T(8,128)(2,1)S(1)} %get-tuple-element.56.refs_0_.refs_16_), channel_id=1, source_target_pairs={{0,16},{8,24},{16,0},{24,8},{1,17},{9,25},{17,1},{25,9},{2,18},{10... | collective-permute-start | bytes 1572872 | tf_op jit(solution)/shard_map/ppermute | solution.py:227
  138.5 31.2 %collective-permute-start.11 = (bf16[8,2,128,128]{3,2,1,0:T(8,128)(2,1)}, bf16[8,2,128,128]{3,2,1,0:T(8,128)(2,1)}, u32[]{:S(2)}, u32[]{:S(2)}) collective-permute-start(bf16[8,2,128,128]{3,2,1,0:T(8,128)(2,1)} %collective-permute-done.10.refs_6_.refs_10_), channel_id=1, source_target_pairs={{0,8},{8,0},{16,24},{24,16},{1,9},{9,1},{17,25},{25,17},{2,10},{10... | collective-permute-start | bytes 1572872 | tf_op jit(solution)/shard_map/ppermute | solution.py:227
  149.7 27.4 %collective-permute-start.21 = (bf16[8,2,128,128]{3,2,1,0:T(8,128)(2,1)S(1)}, bf16[8,2,128,128]{3,2,1,0:T(8,128)(2,1)}, u32[]{:S(2)}, u32[]{:S(2)}) collective-permute-start(bf16[8,2,128,128]{3,2,1,0:T(8,128)(2,1)S(1)} %get-tuple-element.52.refs_4_.refs_16_), channel_id=1, source_target_pairs={{0,8},{8,0},{16,24},{24,16},{1,9},{9,1},{17,25},{25,17},{2,10},{10... | collective-permute-start | bytes 1572872 | tf_op jit(solution)/shard_map/ppermute | solution.py:227
  150.0 27.1 %collective-permute-start.20 = (bf16[8,2,128,128]{3,2,1,0:T(8,128)(2,1)}, bf16[8,2,128,128]{3,2,1,0:T(8,128)(2,1)}, u32[]{:S(2)}, u32[]{:S(2)}) collective-permute-start(bf16[8,2,128,128]{3,2,1,0:T(8,128)(2,1)} %collective-permute-done.18.refs_1_.refs_17_), channel_id=1, source_target_pairs={{0,16},{8,24},{16,0},{24,8},{1,17},{9,25},{17,1},{25,9},{2,18},{10... | collective-permute-start | bytes 1572872 | tf_op jit(solution)/shard_map/ppermute | solution.py:227
  151.9 25.3 %collective-permute-start.23 = (bf16[8,2,128,128]{3,2,1,0:T(8,128)(2,1)}, bf16[8,2,128,128]{3,2,1,0:T(8,128)(2,1)}, u32[]{:S(2)}, u32[]{:S(2)}) collective-permute-start(bf16[8,2,128,128]{3,2,1,0:T(8,128)(2,1)} %collective-permute-done.22.refs_6_.refs_18_), channel_id=1, source_target_pairs={{0,8},{8,0},{16,24},{24,16},{1,9},{9,1},{17,25},{25,17},{2,10},{10... | collective-permute-start | bytes 1572872 | tf_op jit(solution)/shard_map/ppermute | solution.py:227
  196.5 114.7 %reduce-scatter.5.cloned.1.call-start = ((), (), s32[]{:S(2)}) async-start(), calls=%async_computation.5 | async-start | bytes 3538944 | tf_op jit(solution)/shard_map/reduce_scatter | solution.py:278
  220.6 40.2 %collective-permute-start.28 = (bf16[2,8,2,128,128]{4,3,2,1,0:T(8,128)(2,1)}, bf16[2,8,2,128,128]{4,3,2,1,0:T(8,128)(2,1)S(1)}, u32[]{:S(2)}, u32[]{:S(2)}) collective-permute-start(bf16[2,8,2,128,128]{4,3,2,1,0:T(8,128)(2,1)} %get-tuple-element.30), channel_id=1, source_target_pairs={{0,16},{8,24},{16,0},{24,8},{1,17},{9,25},{17,1},{25,9},{2,18},{10... | collective-permute-start | bytes 3145736 | tf_op jit(solution)/shard_map/ppermute | solution.py:227
  233.2 36.2 %collective-permute-start.27 = (bf16[2,8,2,128,128]{4,3,2,1,0:T(8,128)(2,1)}, bf16[2,8,2,128,128]{4,3,2,1,0:T(8,128)(2,1)S(1)}, u32[]{:S(2)}, u32[]{:S(2)}) collective-permute-start(bf16[2,8,2,128,128]{4,3,2,1,0:T(8,128)(2,1)} %get-tuple-element.41), channel_id=1, source_target_pairs={{0,16},{8,24},{16,0},{24,8},{1,17},{9,25},{17,1},{25,9},{2,18},{10... | collective-permute-start | bytes 3145736 | tf_op jit(solution)/shard_map/ppermute | solution.py:227
  246.7 45.2 %collective-permute-start.26 = (bf16[2,8,2,128,128]{4,3,2,1,0:T(8,128)(2,1)}, bf16[2,8,2,128,128]{4,3,2,1,0:T(8,128)(2,1)S(1)}, u32[]{:S(2)}, u32[]{:S(2)}) collective-permute-start(bf16[2,8,2,128,128]{4,3,2,1,0:T(8,128)(2,1)} %get-tuple-element.37), channel_id=1, source_target_pairs={{0,16},{8,24},{16,0},{24,8},{1,17},{9,25},{17,1},{25,9},{2,18},{10... | collective-permute-start | bytes 3145736 | tf_op jit(solution)/shard_map/ppermute | solution.py:227
  259.3 49.0 %collective-permute-start.25 = (bf16[2,8,2,128,128]{4,3,2,1,0:T(8,128)(2,1)}, bf16[2,8,2,128,128]{4,3,2,1,0:T(8,128)(2,1)}, u32[]{:S(2)}, u32[]{:S(2)}) collective-permute-start(bf16[2,8,2,128,128]{4,3,2,1,0:T(8,128)(2,1)} %get-tuple-element.34), channel_id=1, source_target_pairs={{0,16},{8,24},{16,0},{24,8},{1,17},{9,25},{17,1},{25,9},{2,18},{10... | collective-permute-start | bytes 3145736 | tf_op jit(solution)/shard_map/ppermute | solution.py:227
  (32 other events, 1692.9 us)
Sparse Core Ops, SparseCore 0:
  10.3 67.4 all-gather.2
  79.4 63.3 all-gather.4
  196.6 39.8 reduce-scatter.2
  239.2 39.4 reduce-scatter.4
